TPU v7x, 128 devices: a whole 4x4x4 slice. The times are simulated.
128 devices in a mesh: grp: 4 (over y), neg: 32 (over z, x, core).
Axes of the slice: x: 4, y: 4, z: 4, core: 2. Of those that a mesh axis runs over, the one named last changes fastest.
Arguments:
- quotient: bfloat16 [1048576, 256], P(('grp', 'neg')), may hold values from -3 to 3
- remainder: bfloat16 [20480, 256], P(('grp', 'neg')), may hold values from -3 to 3
- request_q: int32 [128, 128, 80], P(('grp', 'neg')), may hold values from -1 to 8191, as said below
- request_r: int32 [128, 128, 24], P(('grp', 'neg')), may hold values from -1 to 159, as said below
- query_q: int32 [32768, 16], P(('grp', 'neg')), may hold values from 0 to 10239, as said below
- query_r: int32 [32768, 16], P(('grp', 'neg')), may hold values from 0 to 3071, as said below
- item_q: int32 [32768, 16], P(('grp', 'neg')), may hold values from 0 to 10239, as said below
- item_r: int32 [32768, 16], P(('grp', 'neg')), may hold values from 0 to 3071, as said below
- positive: int32 [32768], P(('grp', 'neg')), may hold values from 0 to 8191
- query_w1: bfloat16 [256, 1024], replicated, may hold values from -0.375 to 0.375
- query_w2: bfloat16 [1024, 1024], replicated, may hold values from -0.1875 to 0.1875
- query_w3: bfloat16 [1024, 256], replicated, may hold values from -0.1875 to 0.1875
- item_w1: bfloat16 [256, 1024], replicated, may hold values from -0.375 to 0.375
- item_w2: bfloat16 [1024, 1024], replicated, may hold values from -0.1875 to 0.1875
- item_w3: bfloat16 [1024, 256], replicated, may hold values from -0.1875 to 0.1875
Outputs:
- grad_quotient: float32 [1048576, 256], P(('grp', 'neg'))
- grad_remainder: float32 [20480, 256], P(('grp', 'neg'))
- grad_query_w1: bfloat16 [256, 1024], replicated
- grad_query_w2: bfloat16 [1024, 1024], replicated
- grad_query_w3: bfloat16 [1024, 256], replicated
- grad_item_w1: bfloat16 [256, 1024], replicated
- grad_item_w2: bfloat16 [1024, 1024], replicated
- grad_item_w3: bfloat16 [1024, 256], replicated
Inputs may be any that keep to these rules, and one draw needn't show every extreme that they name: `request_q`: for device d and owner p, the first c(d, p) slots hold distinct rows of owner p's shard and the rest hold -1; c(d, p) runs from 26 to 80; in every draw one owner gets 80 rows from every device, and every device asks 80 rows of some owner. `request_r`: for device d and owner p, the first c(d, p) slots hold distinct rows of owner p's shard and the rest hold -1; c(d, p) runs from 1 to 24; in every draw one owner gets 24 rows from every device, and every device asks 24 rows of some owner. `query_q`: entry p * 80 + k names slot k of owner p in request_q of the device holding the example, and that slot is not -1. `query_r`: entry p * 24 + k names slot k of owner p in request_r of the device holding the example, and that slot is not -1. `item_q`: as for query_q. `item_r`: as for query_r.
All inputs are finite; a program needn't handle non-finite values.
Results may differ from a plain program's by a relative error of at most 0.023.
Values may be sent and summed in bfloat16 or wider, within the bound.
No kernel may reach another device: no remote copies, remote signals or barrier semaphores. Data moves between devices by JAX's collectives and lax.ppermute only.
A program may use at most 128 MiB of HBM per device.

v0:
```python
import functools

import jax
import jax.numpy as jnp
from jax import lax
from jax.experimental import pallas as pl
from jax.experimental.pallas import tpu as pltpu
from jax.sharding import Mesh
from jax.sharding import PartitionSpec as P

SCALE = 20.0
EPS = 1e-06
GROUP_AXES = ("z", "x", "core")
MESH_AXES = ("grp", "z", "x", "core")
CHIP_AXES = ("grp", "z", "x")
CORES = [(0, 1), (1, 0)]
VMEM_LIMIT = 60 * 1024 * 1024
HALF = 128


def inner(left, right):
    return lax.dot_general(
        left, right, (((0,), (0,)), ((), ())), preferred_element_type=jnp.float32
    )


def outer_t(left, right):
    return lax.dot_general(
        left, right, (((1,), (1,)), ((), ())), preferred_element_type=jnp.float32
    )


def gelu_back(pre_value, upstream):
    return jax.vjp(jax.nn.gelu, pre_value)[1](upstream)[0]


def tower_forward(pooled, first, second, third):
    pre_one = jnp.dot(pooled, first, preferred_element_type=jnp.float32)
    act_one = jax.nn.gelu(pre_one).astype(jnp.bfloat16)
    pre_two = jnp.dot(act_one, second, preferred_element_type=jnp.float32)
    act_two = jax.nn.gelu(pre_two).astype(jnp.bfloat16)
    vector = jnp.dot(act_two, third, preferred_element_type=jnp.float32)
    inv_norm = lax.rsqrt(jnp.sum(vector * vector, axis=1, keepdims=True) + EPS)
    unit_vec = (vector * inv_norm).astype(jnp.bfloat16)
    return (unit_vec, (pre_one, act_one, pre_two, act_two, vector, inv_norm))


def tower_backward(d_unit, saved, first, second, third):
    pre_one, act_one, pre_two, act_two, vector, inv_norm = saved
    along = jnp.sum(vector * d_unit, axis=1, keepdims=True)
    cubed = inv_norm * inv_norm * inv_norm
    d_vector = (inv_norm * d_unit - cubed * vector * along).astype(jnp.bfloat16)
    d_pre_two = gelu_back(pre_two, outer_t(d_vector, third)).astype(jnp.bfloat16)
    d_pre_one = gelu_back(pre_one, outer_t(d_pre_two, second)).astype(jnp.bfloat16)
    return outer_t(d_pre_one, first), (d_pre_one, d_pre_two, d_vector)


def weight_grads(pooled, saved, backs):
    act_one, act_two = saved[1], saved[3]
    d_pre_one, d_pre_two, d_vector = backs
    grads = (inner(act_one, d_pre_two), inner(act_two, d_vector), inner(d_pre_one, pooled))
    return jnp.concatenate([g.astype(jnp.bfloat16) for g in grads], axis=1)


def score_weights(left, right):
    return jnp.exp(SCALE * outer_t(left, right) - SCALE)


def gather_group(values):
    return lax.all_gather(values, GROUP_AXES, axis=0, tiled=True)


def exchange(rows):
    return lax.all_to_all(rows, MESH_AXES, split_axis=0, concat_axis=0, tiled=True)


def core_sum(grads):
    core, half = lax.axis_index("core"), grads.shape[0] // 2
    kept = lax.dynamic_slice_in_dim(grads, core * half, half, 0)
    given = lax.dynamic_slice_in_dim(grads, (1 - core) * half, half, 0)
    got = lax.ppermute(given, "core", CORES)
    chips = lax.axis_size(CHIP_AXES)
    both = kept.astype(jnp.float32) + got.astype(jnp.float32)
    return both.astype(jnp.bfloat16).reshape(chips, half // chips, -1)


def chip_sum(terms):
    terms = lax.all_to_all(terms, CHIP_AXES, split_axis=0, concat_axis=0, tiled=True)
    return jnp.sum(terms.astype(jnp.float32), axis=0).astype(jnp.bfloat16)


def gather_rows(part):
    return lax.all_gather(part, ("core", *CHIP_AXES), axis=0, tiled=True)


def cost(microseconds):
    return pl.CostEstimate(flops=0, bytes_accessed=int(microseconds * 3.6e6), transcendentals=0)


def whole(space=pltpu.VMEM):
    return pl.BlockSpec(memory_space=space)


def params():
    return pltpu.CompilerParams(vmem_limit_bytes=VMEM_LIMIT)


def loop(count, step, body):
    def run(i, carry):
        body(pl.multiple_of(i * step, step))
        return carry

    lax.fori_loop(0, count // step, run, 0)


def row(place):
    return pl.ds(pl.multiple_of(place, 2), 2)


def halves(first, rows):
    place = pl.multiple_of(2 * first, 16)
    return pl.ds(place, rows, stride=2), pl.ds(place + 1, rows, stride=2)


def widen(narrow_ref, wide_ref, step=64):
    def body(first):
        value = narrow_ref[pl.ds(first, step), :].astype(jnp.float32)
        left, right = halves(first, step)
        wide_ref[left, :] = value[:, :HALF]
        wide_ref[right, :] = value[:, HALF:]

    loop(narrow_ref.shape[0], step, body)


def joined(wide_ref, first, rows):
    left, right = halves(first, rows)
    return jnp.concatenate([wide_ref[left, :], wide_ref[right, :]], axis=1)


def clear(*refs):
    def body(first):
        for ref in refs:
            ref[pl.ds(first, 128), :] = jnp.zeros((128, HALF), jnp.float32)

    loop(refs[0].shape[0], 128, body)


def pick_kernel(place_ref, table_ref, out_ref, wide_ref, stage_ref):
    rows = out_ref.shape[0]
    group = stage_ref.shape[0] // 2
    chunk = pl.program_id(0)

    @pl.when(chunk == 0)
    def _():
        widen(table_ref, wide_ref)

    def body(first):
        places = place_ref.at[pl.ds(chunk * rows + first, group)]
        for j in range(group):
            stage_ref[pl.ds(2 * j, 2), :] = wide_ref[row(places[j]), :]
        out_ref[pl.ds(first, group), :] = joined(stage_ref, 0, group).astype(jnp.bfloat16)

    loop(rows, group, body)


def pick_rows(index, table, chunk=2048, group=64):
    count, (held, features) = index.shape[0], table.shape
    return pl.pallas_call(
        pick_kernel,
        grid=(count // chunk,),
        out_shape=jax.ShapeDtypeStruct((count, features), jnp.bfloat16),
        in_specs=[whole(pltpu.SMEM), whole()],
        out_specs=pl.BlockSpec((chunk, features), lambda i: (i, 0)),
        scratch_shapes=[
            pltpu.VMEM((2 * held, HALF), jnp.float32),
            pltpu.VMEM((2 * group, HALF), jnp.float32),
        ],
        compiler_params=params(),
        cost_estimate=cost(12),
        name="pick_rows",
    )(2 * index, table)


def pool_kernel(place_q_ref, place_r_ref, table_q_ref, table_r_ref, out_ref, wide_q, wide_r, stage_ref):
    widen(table_r_ref, wide_r)
    widen(table_q_ref, wide_q)
    examples = out_ref.shape[0]
    bag = place_q_ref.shape[0] // examples
    group = stage_ref.shape[0] // 2

    def body(first):
        for j in range(group):
            bag_at = pl.ds((first + j) * bag, bag)
            places_q, places_r = place_q_ref.at[bag_at], place_r_ref.at[bag_at]
            terms = [
                wide_q[row(places_q[l]), :] * wide_r[row(places_r[l]), :] for l in range(bag)
            ]
            while len(terms) > 1:
                terms = [a + b for a, b in zip(terms[::2], terms[1::2], strict=True)]
            stage_ref[pl.ds(2 * j, 2), :] = terms[0]
        out_ref[pl.ds(first, group), :] = joined(stage_ref, 0, group).astype(jnp.bfloat16)

    loop(examples, group, body)


def pool_rows(slot_q, slot_r, table_q, table_r, examples, group=16):
    features = table_q.shape[1]
    return pl.pallas_call(
        pool_kernel,
        out_shape=jax.ShapeDtypeStruct((examples, features), jnp.bfloat16),
        in_specs=[whole(pltpu.SMEM), whole(pltpu.SMEM), whole(), whole()],
        out_specs=whole(),
        scratch_shapes=[
            pltpu.VMEM((2 * table_q.shape[0], HALF), jnp.float32),
            pltpu.VMEM((2 * table_r.shape[0], HALF), jnp.float32),
            pltpu.VMEM((2 * group, HALF), jnp.float32),
        ],
        compiler_params=params(),
        cost_estimate=cost(18),
        name="pool_rows",
    )(2 * slot_q, 2 * slot_r, table_q, table_r)


def spread_kernel(place_ref, other_place_ref, other_ref, back_ref, out_ref, wide_ref, back_wide, *totals):
    widen(other_ref, wide_ref)
    widen(back_ref, back_wide)
    clear(*totals)
    examples = back_ref.shape[0]
    bag = place_ref.shape[0] // examples
    share = examples // len(totals)

    def body(e):
        lanes = []
        for lane, total in enumerate(totals):
            example = lane * share + e
            bag_at = pl.ds(example * bag, bag)
            back = back_wide[row(2 * example), :]
            lanes.append((total, back, place_ref.at[bag_at], other_place_ref.at[bag_at]))
        for l in range(bag):
            for total, back, places, other_places in lanes:
                at = row(places[l])
                total[at, :] = total[at, :] + back * wide_ref[row(other_places[l]), :]

    loop(share, 1, body)

    def finish(first):
        value = joined(totals[0], first, 64)
        for total in totals[1:]:
            value = value + joined(total, first, 64)
        out_ref[pl.ds(first, 64), :] = value.astype(jnp.bfloat16)

    loop(out_ref.shape[0], 64, finish)


def spread_rows(slot, other_slot, other, back, rows, estimate, lanes=4):
    features = other.shape[1]
    return pl.pallas_call(
        spread_kernel,
        out_shape=jax.ShapeDtypeStruct((rows, features), jnp.bfloat16),
        in_specs=[whole(pltpu.SMEM), whole(pltpu.SMEM), whole(), whole()],
        out_specs=whole(),
        scratch_shapes=[
            pltpu.VMEM((2 * other.shape[0], HALF), jnp.float32),
            pltpu.VMEM((2 * back.shape[0], HALF), jnp.float32),
        ]
        + [pltpu.VMEM((2 * rows, HALF), jnp.float32)] * lanes,
        compiler_params=params(),
        cost_estimate=cost(estimate),
        name="spread_rows",
    )(2 * slot, 2 * other_slot, other, back)


def absorb_kernel(steps, batch, unroll, place_ref, received_ref, out_ref, total_ref, wide_ref):
    chunk = pl.program_id(0)

    @pl.when(chunk == 0)
    def _():
        clear(total_ref)

    @pl.when(chunk < steps)
    def _():
        widen(received_ref, wide_ref)
        rows = received_ref.shape[0]

        def body(first):
            for start in range(0, unroll, batch):
                places = place_ref.at[pl.ds(chunk * rows + first + start, batch)]
                at = [row(places[j]) for j in range(batch)]
                values = [
                    total_ref[at[j], :] + wide_ref[row(2 * (first + start + j)), :]
                    for j in range(batch)
                ]
                for j in reversed(range(batch)):
                    total_ref[at[j], :] = values[j]

        loop(rows, unroll, body)

    @pl.when(chunk >= steps)
    def _():
        base = pl.multiple_of((chunk - steps) * out_ref.shape[0], out_ref.shape[0])

        def finish(first):
            out_ref[pl.ds(first, 64), :] = joined(total_ref, base + first, 64)

        loop(out_ref.shape[0], 64, finish)


def absorb_rows(index, received, held, batch=16, unroll=80):
    count, features = received.shape
    chunk, block = 2560, 2048
    steps = count // chunk
    return pl.pallas_call(
        functools.partial(absorb_kernel, steps, batch, unroll),
        grid=(steps + held // block,),
        out_shape=jax.ShapeDtypeStruct((held, features), jnp.float32),
        in_specs=[
            whole(pltpu.SMEM),
            pl.BlockSpec((chunk, features), lambda i: (jnp.minimum(i, steps - 1), 0)),
        ],
        out_specs=pl.BlockSpec((block, features), lambda i: (jnp.maximum(i - steps, 0), 0)),
        scratch_shapes=[
            pltpu.VMEM((2 * held, HALF), jnp.float32),
            pltpu.VMEM((2 * chunk, HALF), jnp.float32),
        ],
        compiler_params=params(),
        cost_estimate=cost(22),
        name="absorb_rows",
    )(2 * index, received)


def local(
    quotient,
    remainder,
    request_q,
    request_r,
    query_q,
    query_r,
    item_q,
    item_r,
    positive,
    query_w1,
    query_w2,
    query_w3,
    item_w1,
    item_w2,
    item_w3,
):
    features = quotient.shape[1]
    capacity_q = request_q.shape[2]
    examples = query_q.shape[0]
    lists = request_q.shape[1]
    capacity = capacity_q + request_r.shape[2]
    group = lists // lax.axis_size("grp")
    asked = exchange(
        jnp.concatenate(
            [request_q[0], request_r[0], jnp.broadcast_to(positive[None, :], (lists, examples))],
            axis=1,
        )
    )
    asked_q = jnp.maximum(asked[:, :capacity_q], 0).reshape(-1)
    asked_r = asked[:, capacity_q:capacity].reshape(-1)
    positive_all = lax.dynamic_slice_in_dim(
        asked[:, capacity:], lax.axis_index("grp") * group, group, 0
    ).reshape(1, -1)
    shard_r = remainder.shape[0]
    named_r = (asked_r[:, None] == jnp.arange(shard_r, dtype=jnp.int32)[None, :]).astype(
        jnp.bfloat16
    )
    served_r = jnp.dot(named_r, remainder, preferred_element_type=jnp.float32).astype(jnp.bfloat16)
    served_q = pick_rows(asked_q, quotient)
    table_r = exchange(served_r.reshape(lists, -1, features)).reshape(-1, features)
    table_q = exchange(served_q.reshape(lists, -1, features)).reshape(-1, features)

    slots_iq, slots_ir = item_q.reshape(-1), item_r.reshape(-1)
    slots_qq, slots_qr = query_q.reshape(-1), query_r.reshape(-1)
    slots_q = jnp.concatenate([slots_qq, slots_iq])
    slots_r = jnp.concatenate([slots_qr, slots_ir])
    pooled = pool_rows(slots_q, slots_r, table_q, table_r, 2 * examples)
    pooled_query, pooled_item = pooled[:examples], pooled[examples:]
    query_unit, query_saved = tower_forward(pooled_query, query_w1, query_w2, query_w3)
    item_unit, item_saved = tower_forward(pooled_item, item_w1, item_w2, item_w3)
    units = jnp.concatenate([item_unit, query_unit], axis=1)
    units_all = gather_group(units)
    items_all, queries_all = units_all[:, :features], units_all[:, features:]

    columns = jnp.arange(items_all.shape[0], dtype=jnp.int32)[None, :]
    weights = score_weights(query_unit, items_all)
    inverse = 1.0 / jnp.sum(weights, axis=1, keepdims=True)
    target = (positive[:, None] == columns).astype(jnp.float32)
    d_query = SCALE * jnp.dot(
        (weights * inverse - target).astype(jnp.bfloat16),
        items_all,
        preferred_element_type=jnp.float32,
    )
    inverse_all = lax.all_to_all(
        jnp.broadcast_to(inverse[:, 0][None, :], (group, examples)),
        GROUP_AXES,
        split_axis=0,
        concat_axis=0,
        tiled=True,
    ).reshape(1, -1)
    query_back, query_backs = tower_backward(d_query, query_saved, query_w1, query_w2, query_w3)
    inverse_all, query_backs = lax.optimization_barrier((inverse_all, query_backs))
    query_terms = core_sum(weight_grads(pooled_query, query_saved, query_backs))
    inverse_all, query_terms = lax.optimization_barrier((inverse_all, query_terms))
    query_part = chip_sum(query_terms)
    own = lax.axis_index(GROUP_AXES) * examples + jnp.arange(examples, dtype=jnp.int32)
    weights_t = score_weights(item_unit, queries_all)
    target_t = (positive_all == own[:, None]).astype(jnp.float32)
    d_item = SCALE * jnp.dot(
        (weights_t * inverse_all - target_t).astype(jnp.bfloat16),
        queries_all,
        preferred_element_type=jnp.float32,
    )
    item_back, item_backs = tower_backward(d_item, item_saved, item_w1, item_w2, item_w3)
    item_grads = weight_grads(pooled_item, item_saved, item_backs)
    item_grads, query_part = lax.optimization_barrier((item_grads, query_part))
    query_sum = gather_rows(query_part)
    item_terms = core_sum(item_grads)
    back_all = jnp.concatenate([query_back, item_back], axis=0)
    back_all, item_terms = lax.optimization_barrier((back_all, item_terms))
    item_part = chip_sum(item_terms)
    sums_q = spread_rows(slots_q, slots_r, table_r, back_all, table_q.shape[0], 25)
    sums_q, item_part = lax.optimization_barrier((sums_q, item_part))
    back_q = exchange(sums_q.reshape(lists, -1, features)).reshape(-1, features)
    sums_r = spread_rows(slots_r, slots_q, table_q, back_all, table_r.shape[0], 25)
    item_part, query_sum = lax.optimization_barrier((item_part, query_sum))
    item_sum = gather_rows(item_part)
    back_q, sums_r = lax.optimization_barrier((back_q, sums_r))
    back_r = exchange(sums_r.reshape(lists, -1, features)).reshape(-1, features)
    grad_quotient = absorb_rows(asked_q, back_q, quotient.shape[0])
    grad_quotient, back_r, item_sum = lax.optimization_barrier((grad_quotient, back_r, item_sum))
    grad_remainder = inner(named_r, back_r)
    hidden = query_w2.shape[0]
    weights_out = []
    for summed in (query_sum, item_sum):
        second, third, first_t = jnp.split(summed, [hidden, hidden + features], axis=1)
        weights_out += [first_t.T, second, third]
    return (grad_quotient, grad_remainder, *weights_out)


def solution(mesh):
    cores = Mesh(mesh.devices.reshape(4, 4, 4, 2), MESH_AXES)
    rows = P(MESH_AXES)
    return jax.shard_map(
        local,
        mesh=cores,
        in_specs=(rows,) * 9 + (P(),) * 6,
        out_specs=(rows,) * 2 + (P(),) * 6,
        check_vma=False,
    )
```

profile of v0, /device:TPU:1, one launch (start us, length us, event | category | flops | bytes accessed | tf_op | source)
XLA Modules:
  0.0 500.3 jit_solution(12980623388737132306)
XLA Ops:
  8.1 0.9 add_bitcast_fusion
  9.2 21.7 %all_to_all.48 = s32[128,1,360]{2,1,0:T(1,128)S(1)} all-to-all(s32[128,1,360]{2,1,0:T(1,128)S(1)} %copy.72), channel_id=1, replica_groups=mesh['grp'=4,'z'=4,'x'=4,'core'=2] {'grp','z','x','core'}, dimensions={0} | all-to-all | bytes 368640 | tf_op jit(solution)/shard_map/all_to_all | solution.py:74
  31.3 3.1 convolution_convert_fusion
  34.3 5.1 %all-to-all-start.1 = ((bf16[128,24,256]{2,1,0:T(8,128)(2,1)}), bf16[128,24,256]{2,1,0:T(8,128)(2,1)}, u32[]{:S(2)}, u32[]{:S(2)}) async-start(bf16[128,24,256]{2,1,0:T(8,128)(2,1)} %bitcast.54), calls=%async_computation.1 | async-start | bytes 3145728 | tf_op jit(solution)/shard_map/all_to_all | solution.py:74
  40.3 14.9 %pick_rows.1 = bf16[10240,256]{1,0:T(8,128)(2,1)} custom-call(s32[10240]{0:T(1024)} %mul.351.place_ref, bf16[8192,256]{1,0:T(8,128)(2,1)} %table_ref.1), custom_call_target="tpu_custom_call" | custom-call | bytes 43200000 | tf_op jit(solution)/shard_map/pick_rows/pallas_call | solution.py:168
  55.2 9.0 %all-to-all-done.1 = bf16[128,24,256]{2,1,0:T(8,128)(2,1)} async-done(((bf16[128,24,256]{2,1,0:T(8,128)(2,1)}), bf16[128,24,256]{2,1,0:T(8,128)(2,1)}, u32[]{:S(2)}, u32[]{:S(2)}) %all-to-all-start.1) | async-done | bytes 1572896 | tf_op jit(solution)/shard_map/all_to_all | solution.py:74
  64.2 5.6 %all-to-all-start.2 = ((bf16[128,80,256]{2,1,0:T(8,128)(2,1)}), bf16[128,80,256]{2,1,0:T(8,128)(2,1)}, u32[]{:S(2)}, u32[]{:S(2)}) async-start(bf16[128,80,256]{2,1,0:T(8,128)(2,1)} %bitcast.51), calls=%async_computation.2 | async-start | bytes 10485760 | tf_op jit(solution)/shard_map/all_to_all | solution.py:74
  71.4 62.5 %all-to-all-done.2 = bf16[128,80,256]{2,1,0:T(8,128)(2,1)} async-done(((bf16[128,80,256]{2,1,0:T(8,128)(2,1)}), bf16[128,80,256]{2,1,0:T(8,128)(2,1)}, u32[]{:S(2)}, u32[]{:S(2)}) %all-to-all-start.2) | async-done | bytes 5242912 | tf_op jit(solution)/shard_map/all_to_all | solution.py:74
  133.9 18.8 %pool_rows.1 = bf16[512,256]{1,0:T(8,128)(2,1)} custom-call(s32[8192]{0:T(1024)} %get-tuple-element.114.place_q_ref.place_ref.other_place_ref, s32[8192]{0:T(1024)} %get-tuple-element.115.place_r_ref.other_place_ref.place_ref, bf16[10240,256]{1,0:T(8,128)(2,1)} %bitcast.7.table_q_ref.other_ref, bf16[3072,256]{1,0:T(8,128)(2,1)} %bitcast.5.table_r_ref.other_ref), custom_call_target="tpu_custom_call" | custom-call | bytes 64800000 | tf_op jit(solution)/shard_map/pool_rows/pallas_call | solution.py:208
  152.7 1.3 fusion.49
  154.0 1.0 copy-done.17
  154.9 2.5 fusion.58
  162.3 58.5 %all-gather.4.cloned.1.call-done = bf16[8192,512]{0,1:T(8,128)(2,1)} async-done(((bf16[256,512]{0,1:T(8,128)(2,1)}), bf16[8192,512]{0,1:T(8,128)(2,1)}) %all-gather.4.cloned.1.call-update) | async-done | bytes 8388624 | tf_op jit(solution)/shard_map/all_gather | solution.py:70
  220.8 7.7 %fusion.63 = (f32[256]{0:T(256)S(1)}, f32[256,8192]{1,0:T(8,128)}) fusion(bf16[256,256]{0,1:T(8,128)(2,1)S(1)} %multiply_convert_fusion.5, bf16[8192,512]{0,1:T(8,128)(2,1)} %all-gather.4.cloned.1.call-done), kind=kOutput, calls=%fused_computation.116 | convolution fusion | flops 1080033024 | bytes 12715008 | tf_op jit(solution)/shard_map/dot_general | solution.py:28
  229.1 5.7 %all-to-all-start.3 = ((f32[32,1,256]{2,1,0:T(1,128)}), f32[32,1,256]{2,1,0:T(1,128)}, u32[]{:S(2)}, u32[]{:S(2)}) async-start(f32[32,1,256]{2,1,0:T(1,128)} %broadcast_in_dim.5), calls=%async_computation.3 | async-start | bytes 65536 | tf_op jit(solution)/shard_map/all_to_all | solution.py:395
  234.8 6.6 %multiply_reduce_fusion.1 = (f32[256]{0:T(256)S(1)}, f32[256,256]{0,1:T(8,128)S(1)}) fusion(f32[256,256]{0,1:T(8,128)} %copy-done.15, bf16[8192,512]{0,1:T(8,128)(2,1)} %all-gather.4.cloned.1.call-done, f32[256,8192]{1,0:T(8,128)} %get-tuple-element.109, s32[256]{0:T(256)} %param.23, f32[256]{0:T(256)S(1)} %broadcast_divide_fusion), kind=kOutput, calls=%fused_computation.81 | convolution fusion | flops 1084423936 | bytes 13110272 | tf_op jit(solution)/shard_map/dot_general | solution.py:390
  243.2 2.1 fusion.24
  245.3 1.9 convolution_convert_fusion.4
  249.0 1.7 copy-done.2
  251.8 2.7 collective-permute-done
  254.5 2.3 add_convert_fusion.1
  256.9 1.6 copy.80
  258.4 9.9 %all-to-all-start.4 = ((bf16[64,8,1536]{2,1,0:T(8,128)(2,1)}), bf16[64,8,1536]{2,1,0:T(8,128)(2,1)S(1)}, u32[]{:S(2)}, u32[]{:S(2)}) async-start(bf16[64,8,1536]{2,1,0:T(8,128)(2,1)} %bitcast.52), calls=%async_computation.4 | async-start | bytes 3145728 | tf_op jit(solution)/shard_map/all_to_all | solution.py:88
  268.7 6.5 %multiply_reduce_fusion = (f32[256]{0:T(256)S(1)}, f32[256,256]{0,1:T(8,128)S(1)}) fusion(f32[256,256]{0,1:T(8,128)S(1)} %copy-done.14, bf16[8192,512]{0,1:T(8,128)(2,1)} %all-gather.4.cloned.1.call-done, s32[8192]{0:T(1024)S(1)} %bitcast.62, f32[8192]{0:T(1024)} %bitcast.10, s32[256]{0:T(256)S(1)} %iota_add_fusion, f32[256]{0:T(256)S(1)} %copy-done.30), kind=kOutput, calls=%fused_computation.79 | convolution fusion | flops 2162491136 | bytes 9243648 | tf_op jit(solution)/shard_map/dot_general | solution.py:410
  275.3 2.4 fusion.45
  277.8 1.3 fusion.38
  281.3 1.9 pad_maximum_fusion.1
  283.1 8.9 %all-to-all-done.4 = bf16[64,8,1536]{2,1,0:T(8,128)(2,1)S(1)} async-done(((bf16[64,8,1536]{2,1,0:T(8,128)(2,1)}), bf16[64,8,1536]{2,1,0:T(8,128)(2,1)S(1)}, u32[]{:S(2)}, u32[]{:S(2)}) %all-to-all-start.4) | async-done | bytes 1572896 | tf_op jit(solution)/shard_map/all_to_all | solution.py:88
  293.0 1.7 constant_dynamic-slice_fusion
  294.6 2.0 collective-permute-start.1
  298.2 1.5 collective-permute-done.1
  300.3 1.6 copy.82
  301.9 4.7 all-to-all-start.5
  306.5 22.0 %spread_rows.2 = bf16[10240,256]{1,0:T(8,128)(2,1)} custom-call(s32[8192]{0:T(1024)} %get-tuple-element.114.place_q_ref.place_ref.other_place_ref, s32[8192]{0:T(1024)} %get-tuple-element.115.place_r_ref.other_place_ref.place_ref, bf16[3072,256]{1,0:T(8,128)(2,1)} %bitcast.5.table_r_ref.other_ref, f32[512,256]{1,0:T(8,128)} %pad_maximum_fusion.2.back_ref), custom_call_target="tpu_custom_call" | custom-call | bytes 90000000 | tf_op jit(solution)/shard_map/spread_rows/pallas_call | solution.py:257
  328.5 2.0 all-to-all-done.5
  331.4 7.7 %all-to-all-start.6 = ((bf16[128,80,256]{2,1,0:T(8,128)(2,1)}), bf16[128,80,256]{2,1,0:T(8,128)(2,1)}, u32[]{:S(2)}, u32[]{:S(2)}) async-start(bf16[128,80,256]{2,1,0:T(8,128)(2,1)} %bitcast.50), calls=%async_computation.6 | async-start | bytes 10485760 | tf_op jit(solution)/shard_map/all_to_all | solution.py:74
  339.2 71.5 %all-gather.6.cloned.1.call-done = bf16[1024,1536]{1,0:T(8,128)(2,1)} async-done(((bf16[8,1536]{1,0:T(8,128)(2,1)}), bf16[1024,1536]{1,0:T(8,128)(2,1)}) %all-gather.6.cloned.1.call-update) | async-done | bytes 3145744 | tf_op jit(solution)/shard_map/all_gather | solution.py:93
  410.7 18.4 %spread_rows.3 = bf16[3072,256]{1,0:T(8,128)(2,1)} custom-call(s32[8192]{0:T(1024)} %get-tuple-element.115.place_r_ref.other_place_ref.place_ref, s32[8192]{0:T(1024)} %get-tuple-element.114.place_q_ref.place_ref.other_place_ref, bf16[10240,256]{1,0:T(8,128)(2,1)} %bitcast.7.table_q_ref.other_ref, f32[512,256]{1,0:T(8,128)} %pad_maximum_fusion.2.back_ref), custom_call_target="tpu_custom_call" | custom-call | bytes 90000000 | tf_op jit(solution)/shard_map/spread_rows/pallas_call | solution.py:257
  429.2 7.6 %all-to-all-start.7 = ((bf16[128,24,256]{2,1,0:T(8,128)(2,1)}), bf16[128,24,256]{2,1,0:T(8,128)(2,1)S(1)}, u32[]{:S(2)}, u32[]{:S(2)}) async-start(bf16[128,24,256]{2,1,0:T(8,128)(2,1)} %bitcast.53), calls=%async_computation.7 | async-start | bytes 3145728 | tf_op jit(solution)/shard_map/all_to_all | solution.py:74
  436.8 3.1 split.19
  439.9 2.1 fusion.62
  441.9 1.0 copy.83
  442.9 21.6 %absorb_rows.1 = f32[8192,256]{1,0:T(8,128)} custom-call(s32[10240]{0:T(1024)} %mul.351.place_ref, bf16[10240,256]{1,0:T(8,128)(2,1)} %bitcast.13.received_ref), custom_call_target="tpu_custom_call" | custom-call | bytes 79200000 | tf_op jit(solution)/shard_map/absorb_rows/pallas_call | solution.py:312
  464.5 21.8 %all-gather.8.cloned.1.call-done = bf16[1024,1536]{1,0:T(8,128)(2,1)} async-done(((bf16[8,1536]{1,0:T(8,128)(2,1)}), bf16[1024,1536]{1,0:T(8,128)(2,1)}) %all-gather.8.cloned.1.call-update) | async-done | bytes 3145744 | tf_op jit(solution)/shard_map/all_gather | solution.py:93
  486.3 2.2 fusion.61
  488.6 3.1 split.22
  491.6 1.1 fusion.15
  492.7 1.0 copy.84
  (144 shorter events, 20.1 us)
Async XLA Ops:
  7.2 152.2 %copy-start = (bf16[1024,1024]{1,0:T(8,128)(2,1)S(1)}, bf16[1024,1024]{1,0:T(8,128)(2,1)}, u32[]{:S(2)}) copy-start(bf16[1024,1024]{1,0:T(8,128)(2,1)} %param.25) | copy-start | bytes 6291460
  31.0 24.1 %copy-start.22 = (s32[128,1,360]{0,2,1:T(8,128)}, s32[128,1,360]{0,2,1:T(8,128)S(1)}, u32[]{:S(2)}) copy-start(s32[128,1,360]{0,2,1:T(8,128)S(1)} %copy.73) | copy-start | bytes 552964
  34.3 29.9 %all-to-all-start.1 = ((bf16[128,24,256]{2,1,0:T(8,128)(2,1)}), bf16[128,24,256]{2,1,0:T(8,128)(2,1)}, u32[]{:S(2)}, u32[]{:S(2)}) async-start(bf16[128,24,256]{2,1,0:T(8,128)(2,1)} %bitcast.54), calls=%async_computation.1 | async-start | bytes 3145728 | tf_op jit(solution)/shard_map/all_to_all | solution.py:74
  64.2 5.7 %copy-start.24 = (s32[256,16]{0,1:T(8,128)S(1)}, s32[256,16]{0,1:T(8,128)}, u32[]{:S(2)}) copy-start(s32[256,16]{0,1:T(8,128)} %param.19) | copy-start | bytes 49156
  64.2 5.9 %copy-start.25 = (s32[256,16]{0,1:T(8,128)S(1)}, s32[256,16]{0,1:T(8,128)}, u32[]{:S(2)}) copy-start(s32[256,16]{0,1:T(8,128)} %param.20) | copy-start | bytes 49156
  64.2 6.1 %copy-start.26 = (s32[256,16]{0,1:T(8,128)S(1)}, s32[256,16]{0,1:T(8,128)}, u32[]{:S(2)}) copy-start(s32[256,16]{0,1:T(8,128)} %param.21) | copy-start | bytes 49156
  64.2 6.3 %copy-start.27 = (s32[256,16]{0,1:T(8,128)S(1)}, s32[256,16]{0,1:T(8,128)}, u32[]{:S(2)}) copy-start(s32[256,16]{0,1:T(8,128)} %param.22) | copy-start | bytes 49156
  64.2 69.7 %all-to-all-start.2 = ((bf16[128,80,256]{2,1,0:T(8,128)(2,1)}), bf16[128,80,256]{2,1,0:T(8,128)(2,1)}, u32[]{:S(2)}, u32[]{:S(2)}) async-start(bf16[128,80,256]{2,1,0:T(8,128)(2,1)} %bitcast.51), calls=%async_computation.2 | async-start | bytes 10485760 | tf_op jit(solution)/shard_map/all_to_all | solution.py:74
  69.8 151.0 %all-gather.4.cloned.1.call-start = ((), (), s32[]{:S(2)}) async-start(), calls=%async_computation.8 | async-start | bytes 8650752 | tf_op jit(solution)/shard_map/all_gather | solution.py:70
  133.9 18.8 %copy-start.6 = (bf16[256,1024]{1,0:T(8,128)(2,1)S(1)}, bf16[256,1024]{1,0:T(8,128)(2,1)}, u32[]{:S(2)}) copy-start(bf16[256,1024]{1,0:T(8,128)(2,1)} %param.27) | copy-start | bytes 1572868
  152.7 4.7 copy-start.36
  154.9 4.1 copy-start.4
  154.9 4.1 copy-start.5
  158.1 3.4 copy-start.13
  159.0 2.5 copy-start.29
  159.4 1.5 copy-start.19
  160.2 1.4 copy-start.39
  229.1 16.2 %all-to-all-start.3 = ((f32[32,1,256]{2,1,0:T(1,128)}), f32[32,1,256]{2,1,0:T(1,128)}, u32[]{:S(2)}, u32[]{:S(2)}) async-start(f32[32,1,256]{2,1,0:T(1,128)} %broadcast_in_dim.5), calls=%async_computation.3 | async-start | bytes 65536 | tf_op jit(solution)/shard_map/all_to_all | solution.py:395
  234.8 6.7 %copy-start.16 = (f32[256,256]{0,1:T(8,128)S(1)}, f32[256,256]{0,1:T(8,128)}, u32[]{:S(2)}) copy-start(f32[256,256]{0,1:T(8,128)} %copy-done.15) | copy-start | bytes 786436
  234.8 6.7 %copy-start.31 = (f32[256]{0:T(256)S(1)}, f32[256]{0:T(256)}, u32[]{:S(2)}) copy-start(f32[256]{0:T(256)} %get-tuple-element.101) | copy-start | bytes 3076
  234.8 6.7 %copy-start.32 = (f32[256]{0:T(256)S(1)}, f32[256]{0:T(256)}, u32[]{:S(2)}) copy-start(f32[256]{0:T(256)} %get-tuple-element.102) | copy-start | bytes 3076
  234.8 6.7 %copy-start.35 = (bf16[1024,256]{1,0:T(8,128)(2,1)S(1)}, bf16[1024,256]{1,0:T(8,128)(2,1)}, u32[]{:S(2)}) copy-start(bf16[1024,256]{1,0:T(8,128)(2,1)} %param.26) | copy-start | bytes 1572868
  234.8 6.7 %copy-start.40 = (f32[256,1024]{1,0:T(8,128)S(1)}, f32[256,1024]{1,0:T(8,128)}, u32[]{:S(2)}) copy-start(f32[256,1024]{1,0:T(8,128)} %copy-done.39) | copy-start | bytes 3145732
  241.6 1.7 copy-start.20
  245.3 1.9 copy-start.7
  245.3 2.3 copy-start.21
  245.3 2.3 copy-start.42
  249.0 1.7 copy-start.2
  250.8 3.7 collective-permute-start
  256.8 11.8 %copy-start.14 = (f32[256,256]{0,1:T(8,128)S(1)}, f32[256,256]{0,1:T(8,128)}, u32[]{:S(2)}) copy-start(f32[256,256]{0,1:T(8,128)} %copy-done.13) | copy-start | bytes 786436
  256.9 11.8 %copy-start.30 = (f32[256]{0:T(256)S(1)}, f32[256]{0:T(256)}, u32[]{:S(2)}) copy-start(f32[256]{0:T(256)} %copy-done.29) | copy-start | bytes 3076
  258.4 33.6 %all-to-all-start.4 = ((bf16[64,8,1536]{2,1,0:T(8,128)(2,1)}), bf16[64,8,1536]{2,1,0:T(8,128)(2,1)S(1)}, u32[]{:S(2)}, u32[]{:S(2)}) async-start(bf16[64,8,1536]{2,1,0:T(8,128)(2,1)} %bitcast.52), calls=%async_computation.4 | async-start | bytes 3145728 | tf_op jit(solution)/shard_map/all_to_all | solution.py:88
  268.4 142.3 %all-gather.6.cloned.1.call-start = ((), (), s32[]{:S(2)}) async-start(), calls=%async_computation.9 | async-start | bytes 3170304 | tf_op jit(solution)/shard_map/all_gather | solution.py:93
  268.7 6.6 %copy-start.28 = (f32[256]{0:T(256)S(1)}, f32[256]{0:T(256)}, u32[]{:S(2)}) copy-start(f32[256]{0:T(256)} %get-tuple-element.99) | copy-start | bytes 3076
  275.3 2.4 copy-start.18
  275.3 2.4 copy-start.33
  277.8 2.1 copy-start.38
  283.1 13.5 %copy-start.8 = (bf16[256,1024]{1,0:T(8,128)(2,1)S(1)}, bf16[256,1024]{1,0:T(8,128)(2,1)}, u32[]{:S(2)}) copy-start(bf16[256,1024]{1,0:T(8,128)(2,1)} %fusion.24) | copy-start | bytes 1572868
  292.9 4.1 copy-start.10
  293.0 6.7 %copy-start.3 = (bf16[1024,1536]{0,1:T(8,128)(2,1)S(1)}, bf16[1024,1536]{0,1:T(8,128)(2,1)}, u32[]{:S(2)}) copy-start(bf16[1024,1536]{0,1:T(8,128)(2,1)} %pad_maximum_fusion.1) | copy-start | bytes 9437188
  294.6 5.0 %collective-permute-start.1 = (bf16[512,1536]{0,1:T(8,128)(2,1)S(1)}, bf16[512,1536]{0,1:T(8,128)(2,1)S(1)}, u32[]{:S(2)}, u32[]{:S(2)}) collective-permute-start(bf16[512,1536]{0,1:T(8,128)(2,1)S(1)} %constant_dynamic-slice_fusion), channel_id=1, source_target_pairs={{0,1},{1,0},{2,3},{3,2},{4,5},{5,4},{6,7},{7,6},{8,9},{9,8},{10,11... | collective-permute-start | bytes 4718600 | tf_op jit(solution)/shard_map/ppermute | solution.py:81
  301.9 28.7 %all-to-all-start.5 = ((bf16[64,8,1536]{2,1,0:T(8,128)(2,1)}), bf16[64,8,1536]{2,1,0:T(8,128)(2,1)S(1)}, u32[]{:S(2)}, u32[]{:S(2)}) async-start(bf16[64,8,1536]{2,1,0:T(8,128)(2,1)} %bitcast.55), calls=%async_computation.5 | async-start | bytes 3145728 | tf_op jit(solution)/shard_map/all_to_all | solution.py:88
  331.4 97.8 %all-to-all-start.6 = ((bf16[128,80,256]{2,1,0:T(8,128)(2,1)}), bf16[128,80,256]{2,1,0:T(8,128)(2,1)}, u32[]{:S(2)}, u32[]{:S(2)}) async-start(bf16[128,80,256]{2,1,0:T(8,128)(2,1)} %bitcast.50), calls=%async_computation.6 | async-start | bytes 10485760 | tf_op jit(solution)/shard_map/all_to_all | solution.py:74
  339.1 147.2 %all-gather.8.cloned.1.call-start = ((), (), s32[]{:S(2)}) async-start(), calls=%async_computation.10 | async-start | bytes 3170304 | tf_op jit(solution)/shard_map/all_gather | solution.py:93
  429.2 35.4 %all-to-all-start.7 = ((bf16[128,24,256]{2,1,0:T(8,128)(2,1)}), bf16[128,24,256]{2,1,0:T(8,128)(2,1)S(1)}, u32[]{:S(2)}, u32[]{:S(2)}) async-start(bf16[128,24,256]{2,1,0:T(8,128)(2,1)} %bitcast.53), calls=%async_computation.7 | async-start | bytes 3145728 | tf_op jit(solution)/shard_map/all_to_all | solution.py:74
  464.5 21.8 %copy-start.11 = (bf16[128,24,256]{2,1,0:T(8,128)(2,1)}, bf16[128,24,256]{2,1,0:T(8,128)(2,1)S(1)}, u32[]{:S(2)}) copy-start(bf16[128,24,256]{2,1,0:T(8,128)(2,1)S(1)} %all-to-all-done.7) | copy-start | bytes 4718596
  486.3 5.3 %copy-start.12 = (bf16[128,24,256]{2,1,0:T(8,128)(2,1)S(1)}, bf16[128,24,256]{2,1,0:T(8,128)(2,1)}, u32[]{:S(2)}) copy-start(bf16[128,24,256]{2,1,0:T(8,128)(2,1)} %copy-done.11) | copy-start | bytes 4718596
  486.3 7.4 %copy-start.1 = (bf16[1024,1024]{1,0:T(8,128)(2,1)S(1)}, bf16[1024,1024]{1,0:T(8,128)(2,1)}, u32[]{:S(2)}) copy-start(bf16[1024,1024]{1,0:T(8,128)(2,1)} %param.25) | copy-start | bytes 6291460
  (7 other events, 6.4 us)
Sparse Core Ops, SparseCore 0:
  162.4 58.2 all-gather.3
  293.1 117.5 all-gather.5
  414.4 71.9 all-gather.7
where the time goes:
time: 501 us; the launch traced here: 500 us
  waiting for transfers between devices  239 us (48%)
  Pallas kernels  95.7 us (19%)
  starting transfers between devices  49.3 us (10%)
  matrix products  43.3 us (9%)
  local copies, waits for them, and re-layouts  25.9 us (5%)
  blocking collectives  21.7 us (4%)
  between operations  14.5 us (3%)
  other arithmetic  11.4 us (2%)
    all_gather x2, waiting for transfers between devices, gather_rows(): return lax.all_gather(part, ('core', *CHIP_AXES), axis=0, tiled=True)  93.3 us
    all_to_all x4, waiting for transfers between devices, exchange(): lax.all_to_all(rows, MESH_AXES, split_axis=0, concat_axis=0, tiled=True)  71.6 us
    all_gather x1, waiting for transfers between devices, gather_group(): return lax.all_gather(values, GROUP_AXES, axis=0, tiled=True)  58.5 us
    pallas_call x2, Pallas kernels, spread_rows(): pl.pallas_call(spread_kernel, out_shape=jax.ShapeDtypeStruct((rows, featu...  40.4 us
    all_to_all x4, starting transfers between devices, exchange(): lax.all_to_all(rows, MESH_AXES, split_axis=0, concat_axis=0, tiled=True)  26.1 us
    all_to_all x1, blocking collectives, exchange(): lax.all_to_all(rows, MESH_AXES, split_axis=0, concat_axis=0, tiled=True)  21.7 us
    pallas_call x1, Pallas kernels, absorb_rows(): pl.pallas_call(functools.partial(absorb_kernel, steps, batch, unroll), gr...  21.6 us
    pallas_call x1, Pallas kernels, pool_rows(): pl.pallas_call(pool_kernel, out_shape=jax.ShapeDtypeStruct((examples, fea...  18.8 us
  transfers between devices with their start and end apart: 12, of which 9 were waited for; matrix products, arithmetic and copies ran while one was open for 8% of the time, Pallas kernels for 15%

commit v1 on v0

--- a/solution.py
+++ b/solution.py
@@ -4,6 +4,7 @@
 import jax.numpy as jnp
 from jax import lax
 from jax.experimental import pallas as pl
+from jax.experimental.layout import Layout, with_layout_constraint
 from jax.experimental.pallas import tpu as pltpu
 from jax.sharding import Mesh
 from jax.sharding import PartitionSpec as P
@@ -59,7 +60,8 @@
     act_one, act_two = saved[1], saved[3]
     d_pre_one, d_pre_two, d_vector = backs
     grads = (inner(act_one, d_pre_two), inner(act_two, d_vector), inner(d_pre_one, pooled))
-    return jnp.concatenate([g.astype(jnp.bfloat16) for g in grads], axis=1)
+    joint = jnp.concatenate([g.astype(jnp.bfloat16) for g in grads], axis=1)
+    return with_layout_constraint(joint, Layout(major_to_minor=(0, 1)))
 
 
 def score_weights(left, right):
@@ -349,19 +351,10 @@
     capacity_q = request_q.shape[2]
     examples = query_q.shape[0]
     lists = request_q.shape[1]
-    capacity = capacity_q + request_r.shape[2]
     group = lists // lax.axis_size("grp")
-    asked = exchange(
-        jnp.concatenate(
-            [request_q[0], request_r[0], jnp.broadcast_to(positive[None, :], (lists, examples))],
-            axis=1,
-        )
-    )
+    asked = exchange(jnp.concatenate([request_q[0], request_r[0]], axis=1))
     asked_q = jnp.maximum(asked[:, :capacity_q], 0).reshape(-1)
-    asked_r = asked[:, capacity_q:capacity].reshape(-1)
-    positive_all = lax.dynamic_slice_in_dim(
-        asked[:, capacity:], lax.axis_index("grp") * group, group, 0
-    ).reshape(1, -1)
+    asked_r = asked[:, capacity_q:].reshape(-1)
     shard_r = remainder.shape[0]
     named_r = (asked_r[:, None] == jnp.arange(shard_r, dtype=jnp.int32)[None, :]).astype(
         jnp.bfloat16
@@ -392,49 +385,46 @@
         items_all,
         preferred_element_type=jnp.float32,
     )
-    inverse_all = lax.all_to_all(
-        jnp.broadcast_to(inverse[:, 0][None, :], (group, examples)),
+    told = jnp.stack([inverse[:, 0], positive.astype(jnp.float32)])
+    told_all = lax.all_to_all(
+        jnp.broadcast_to(told[None], (group, *told.shape)),
         GROUP_AXES,
         split_axis=0,
         concat_axis=0,
         tiled=True,
-    ).reshape(1, -1)
+    )
     query_back, query_backs = tower_backward(d_query, query_saved, query_w1, query_w2, query_w3)
-    inverse_all, query_backs = lax.optimization_barrier((inverse_all, query_backs))
+    told_all, query_backs = lax.optimization_barrier((told_all, query_backs))
     query_terms = core_sum(weight_grads(pooled_query, query_saved, query_backs))
-    inverse_all, query_terms = lax.optimization_barrier((inverse_all, query_terms))
-    query_part = chip_sum(query_terms)
+    inverse_all, positive_all = (told_all[:, i, :].reshape(1, -1) for i in range(2))
     own = lax.axis_index(GROUP_AXES) * examples + jnp.arange(examples, dtype=jnp.int32)
     weights_t = score_weights(item_unit, queries_all)
-    target_t = (positive_all == own[:, None]).astype(jnp.float32)
+    target_t = (positive_all == own[:, None].astype(jnp.float32)).astype(jnp.float32)
     d_item = SCALE * jnp.dot(
         (weights_t * inverse_all - target_t).astype(jnp.bfloat16),
         queries_all,
         preferred_element_type=jnp.float32,
     )
     item_back, item_backs = tower_backward(d_item, item_saved, item_w1, item_w2, item_w3)
-    item_grads = weight_grads(pooled_item, item_saved, item_backs)
-    item_grads, query_part = lax.optimization_barrier((item_grads, query_part))
-    query_sum = gather_rows(query_part)
-    item_terms = core_sum(item_grads)
+    item_terms = core_sum(weight_grads(pooled_item, item_saved, item_backs))
     back_all = jnp.concatenate([query_back, item_back], axis=0)
-    back_all, item_terms = lax.optimization_barrier((back_all, item_terms))
-    item_part = chip_sum(item_terms)
+    terms = jnp.concatenate([query_terms, item_terms], axis=2)
+    back_all, terms = lax.optimization_barrier((back_all, terms))
+    part = chip_sum(terms)
     sums_q = spread_rows(slots_q, slots_r, table_r, back_all, table_q.shape[0], 25)
-    sums_q, item_part = lax.optimization_barrier((sums_q, item_part))
+    sums_r = spread_rows(slots_r, slots_q, table_q, back_all, table_r.shape[0], 25)
+    sums_q, sums_r, part = lax.optimization_barrier((sums_q, sums_r, part))
+    summed = gather_rows(part)
     back_q = exchange(sums_q.reshape(lists, -1, features)).reshape(-1, features)
-    sums_r = spread_rows(slots_r, slots_q, table_q, back_all, table_r.shape[0], 25)
-    item_part, query_sum = lax.optimization_barrier((item_part, query_sum))
-    item_sum = gather_rows(item_part)
     back_q, sums_r = lax.optimization_barrier((back_q, sums_r))
     back_r = exchange(sums_r.reshape(lists, -1, features)).reshape(-1, features)
     grad_quotient = absorb_rows(asked_q, back_q, quotient.shape[0])
-    grad_quotient, back_r, item_sum = lax.optimization_barrier((grad_quotient, back_r, item_sum))
+    grad_quotient, back_r, summed = lax.optimization_barrier((grad_quotient, back_r, summed))
     grad_remainder = inner(named_r, back_r)
     hidden = query_w2.shape[0]
     weights_out = []
-    for summed in (query_sum, item_sum):
-        second, third, first_t = jnp.split(summed, [hidden, hidden + features], axis=1)
+    for both in jnp.split(summed, 2, axis=1):
+        second, third, first_t = jnp.split(both, [hidden, hidden + features], axis=1)
         weights_out += [first_t.T, second, third]
     return (grad_quotient, grad_remainder, *weights_out)
 

time: 501 us -> 467 us (0.932)
  waiting for transfers between devices: 239 us -> 160 us
  blocking collectives: 21.7 us -> 94.9 us
  starting transfers between devices: 49.3 us -> 28.1 us
  matrix products: 43.3 us -> 37.4 us
  local copies, waits for them, and re-layouts: 25.9 us -> 20.3 us
    all_to_all x1 -> x2, blocking collectives: 21.7 us -> 94.9 us  [exchange(): lax.all_to_all(rows, MESH_AXES, split_axis=0, concat_axis=0, tiled=True)]
    all_gather x2 -> x1, waiting for transfers between devices: 93.3 us -> 21.6 us  [gather_rows(): return lax.all_gather(part, ('core', *CHIP_AXES), axis=0, tiled=True)]
    all_to_all x4 -> x3, starting transfers between devices: 26.1 us -> 15.3 us  [exchange(): lax.all_to_all(rows, MESH_AXES, split_axis=0, concat_axis=0, tiled=True)]
    all_to_all x2 -> x1, waiting for transfers between devices: 10.9 us -> 0.33 us  [chip_sum(): lax.all_to_all(terms, CHIP_AXES, split_axis=0, concat_axis=0, tiled=True)]
    all_to_all x2 -> x1, starting transfers between devices: 14.6 us -> 6.61 us  [chip_sum(): lax.all_to_all(terms, CHIP_AXES, split_axis=0, concat_axis=0, tiled=True)]
    all_to_all x4 -> x3, waiting for transfers between devices: 71.6 us -> 77.6 us  [exchange(): lax.all_to_all(rows, MESH_AXES, split_axis=0, concat_axis=0, tiled=True)]
    split x4 -> x2, local copies, waits for them, and re-layouts: 10.4 us -> 7.47 us  [local(): jnp.split(both, [hidden, hidden + features], axis=1)]
  transfers between devices with their start and end apart: 12 -> 9, of which waited for: 9 -> 7; matrix products, arithmetic and copies ran while one was open for 8% -> 3% of each run, Pallas kernels for 15% -> 17%
where the time goes in v1:
time: 467 us; the launch traced here: 466 us
  waiting for transfers between devices  160 us (34%)
  Pallas kernels  95.7 us (20%)
  blocking collectives  94.9 us (20%)
  matrix products  37.4 us (8%)
  starting transfers between devices  28.1 us (6%)
  local copies, waits for them, and re-layouts  20.3 us (4%)
  other arithmetic  14.7 us (3%)
  between operations  14.7 us (3%)
    all_to_all x2, blocking collectives, exchange(): lax.all_to_all(rows, MESH_AXES, split_axis=0, concat_axis=0, tiled=True)  94.9 us
    all_to_all x3, waiting for transfers between devices, exchange(): lax.all_to_all(rows, MESH_AXES, split_axis=0, concat_axis=0, tiled=True)  77.6 us
    all_gather x1, waiting for transfers between devices, gather_group(): return lax.all_gather(values, GROUP_AXES, axis=0, tiled=True)  56.6 us
    pallas_call x2, Pallas kernels, spread_rows(): pl.pallas_call(spread_kernel, out_shape=jax.ShapeDtypeStruct((rows, featu...  40.4 us
    pallas_call x1, Pallas kernels, absorb_rows(): pl.pallas_call(functools.partial(absorb_kernel, steps, batch, unroll), gr...  21.6 us
    all_gather x1, waiting for transfers between devices, gather_rows(): return lax.all_gather(part, ('core', *CHIP_AXES), axis=0, tiled=True)  21.6 us
    pallas_call x1, Pallas kernels, pool_rows(): pl.pallas_call(pool_kernel, out_shape=jax.ShapeDtypeStruct((examples, fea...  18.8 us
    all_to_all x3, starting transfers between devices, exchange(): lax.all_to_all(rows, MESH_AXES, split_axis=0, concat_axis=0, tiled=True)  15.3 us
  transfers between devices with their start and end apart: 9, of which 7 were waited for; matrix products, arithmetic and copies ran while one was open for 3% of the time, Pallas kernels for 17%

profile of v1, /device:TPU:1, one launch (start us, length us, event | category | flops | bytes accessed | tf_op | source)
XLA Modules:
  0.0 466.0 jit_solution(7010103499665860206)
XLA Ops:
  7.2 1.0 copy.59
  8.2 0.8 copy.60
  9.1 20.8 %all_to_all.42 = s32[128,1,104]{2,1,0:T(1,128)S(1)} all-to-all(s32[128,1,104]{2,1,0:T(1,128)S(1)} %bitcast.58), channel_id=1, replica_groups=mesh['grp'=4,'z'=4,'x'=4,'core'=2] {'grp','z','x','core'}, dimensions={0} | all-to-all | bytes 106496 | tf_op jit(solution)/shard_map/all_to_all | solution.py:76
  30.1 3.1 convolution_convert_fusion
  33.1 5.3 %all-to-all-start.1 = ((bf16[128,24,256]{2,1,0:T(8,128)(2,1)}), bf16[128,24,256]{2,1,0:T(8,128)(2,1)}, u32[]{:S(2)}, u32[]{:S(2)}) async-start(bf16[128,24,256]{2,1,0:T(8,128)(2,1)} %bitcast.54), calls=%async_computation.1 | async-start | bytes 3145728 | tf_op jit(solution)/shard_map/all_to_all | solution.py:76
  39.2 14.9 %pick_rows.1 = bf16[10240,256]{1,0:T(8,128)(2,1)} custom-call(s32[10240]{0:T(1024)} %mul.348.place_ref, bf16[8192,256]{1,0:T(8,128)(2,1)} %table_ref.1), custom_call_target="tpu_custom_call" | custom-call | bytes 43200000 | tf_op jit(solution)/shard_map/pick_rows/pallas_call | solution.py:170
  54.0 9.2 %all-to-all-done.1 = bf16[128,24,256]{2,1,0:T(8,128)(2,1)} async-done(((bf16[128,24,256]{2,1,0:T(8,128)(2,1)}), bf16[128,24,256]{2,1,0:T(8,128)(2,1)}, u32[]{:S(2)}, u32[]{:S(2)}) %all-to-all-start.1) | async-done | bytes 1572896 | tf_op jit(solution)/shard_map/all_to_all | solution.py:76
  63.2 5.6 %all-to-all-start.2 = ((bf16[128,80,256]{2,1,0:T(8,128)(2,1)}), bf16[128,80,256]{2,1,0:T(8,128)(2,1)}, u32[]{:S(2)}, u32[]{:S(2)}) async-start(bf16[128,80,256]{2,1,0:T(8,128)(2,1)} %bitcast.51), calls=%async_computation.2 | async-start | bytes 10485760 | tf_op jit(solution)/shard_map/all_to_all | solution.py:76
  70.4 62.5 %all-to-all-done.2 = bf16[128,80,256]{2,1,0:T(8,128)(2,1)} async-done(((bf16[128,80,256]{2,1,0:T(8,128)(2,1)}), bf16[128,80,256]{2,1,0:T(8,128)(2,1)}, u32[]{:S(2)}, u32[]{:S(2)}) %all-to-all-start.2) | async-done | bytes 5242912 | tf_op jit(solution)/shard_map/all_to_all | solution.py:76
  132.9 18.8 %pool_rows.1 = bf16[512,256]{1,0:T(8,128)(2,1)} custom-call(s32[8192]{0:T(1024)} %get-tuple-element.92.place_q_ref.place_ref.other_place_ref, s32[8192]{0:T(1024)} %get-tuple-element.93.place_r_ref.other_place_ref.place_ref, bf16[10240,256]{1,0:T(8,128)(2,1)} %bitcast.7.table_q_ref.other_ref, bf16[3072,256]{1,0:T(8,128)(2,1)} %bitcast.5.table_r_ref.other_ref), custom_call_target="tpu_custom_call" | custom-call | bytes 64800000 | tf_op jit(solution)/shard_map/pool_rows/pallas_call | solution.py:210
  151.7 1.3 fusion.51
  153.0 1.0 copy-done.19
  153.9 2.5 fusion.60
  158.3 0.8 fusion.59
  161.3 1.3 convert_element_type.113
  163.2 56.6 %all-gather.3.cloned.1.call-done = bf16[8192,512]{0,1:T(8,128)(2,1)} async-done(((bf16[256,512]{0,1:T(8,128)(2,1)}), bf16[8192,512]{0,1:T(8,128)(2,1)}) %all-gather.3.cloned.1.call-update) | async-done | bytes 8388624 | tf_op jit(solution)/shard_map/all_gather | solution.py:72
  219.8 4.1 fusion.66
  224.5 2.0 multiply_reduce_fusion.1
  226.5 1.7 fusion.33
  228.9 5.6 %all-to-all-start.3 = ((f32[32,2,256]{2,1,0:T(2,128)}), f32[32,2,256]{2,1,0:T(2,128)S(1)}, u32[]{:S(2)}, u32[]{:S(2)}) async-start(f32[32,2,256]{2,1,0:T(2,128)} %broadcast_in_dim.2), calls=%async_computation.3 | async-start | bytes 131072 | tf_op jit(solution)/shard_map/all_to_all | solution.py:389
  234.5 3.4 fusion.26
  237.9 3.9 all-to-all-done.3
  241.9 6.7 %multiply_reduce_fusion = (f32[256]{0:T(256)S(1)}, f32[256,256]{0,1:T(8,128)S(1)}) fusion(f32[256,256]{0,1:T(8,128)} %copy-done.15, bf16[8192,512]{0,1:T(8,128)(2,1)} %all-gather.3.cloned.1.call-done, f32[8192]{0:T(1024)S(1)} %bitcast.62, f32[8192]{0:T(1024)S(1)} %bitcast.61, f32[256]{0:T(256)} %add_convert_fusion.2, f32[256]{0:T(256)} %copy-done.30), kind=kOutput, calls=%fused_computation.82 | convolution fusion | flops 2162491136 | bytes 9243648 | tf_op jit(solution)/shard_map/dot_general | solution.py:403
  248.7 2.2 fusion.47
  251.5 0.9 convolution_convert_fusion.1
  252.5 1.3 fusion.40
  253.9 0.9 convolution_convert_fusion.2
  256.6 1.4 constant_dynamic-slice_fusion.1
  259.0 1.3 constant_dynamic-slice_fusion
  260.3 0.9 copy-done.4
  262.0 0.8 pad_maximum_fusion.3.back_ref
  263.4 1.8 fusion.16
  265.2 1.8 fusion.17
  267.0 2.1 pad_maximum_fusion.2
  269.1 6.6 %all-to-all-start.4 = ((bf16[64,8,3072]{2,1,0:T(8,128)(2,1)}), bf16[64,8,3072]{2,1,0:T(8,128)(2,1)}, u32[]{:S(2)}, u32[]{:S(2)}) async-start(bf16[64,8,3072]{2,1,0:T(8,128)(2,1)} %pad_maximum_fusion.2), calls=%async_computation.4 | async-start | bytes 6291456 | tf_op jit(solution)/shard_map/all_to_all | solution.py:90
  275.8 18.4 %spread_rows.3 = bf16[3072,256]{1,0:T(8,128)(2,1)} custom-call(s32[8192]{0:T(1024)} %get-tuple-element.93.place_r_ref.other_place_ref.place_ref, s32[8192]{0:T(1024)} %get-tuple-element.92.place_q_ref.place_ref.other_place_ref, bf16[10240,256]{1,0:T(8,128)(2,1)} %bitcast.7.table_q_ref.other_ref, f32[512,256]{1,0:T(8,128)} %pad_maximum_fusion.3.back_ref), custom_call_target="tpu_custom_call" | custom-call | bytes 90000000 | tf_op jit(solution)/shard_map/spread_rows/pallas_call | solution.py:259
  294.2 22.0 %spread_rows.2 = bf16[10240,256]{1,0:T(8,128)(2,1)} custom-call(s32[8192]{0:T(1024)} %get-tuple-element.92.place_q_ref.place_ref.other_place_ref, s32[8192]{0:T(1024)} %get-tuple-element.93.place_r_ref.other_place_ref.place_ref, bf16[3072,256]{1,0:T(8,128)(2,1)} %bitcast.5.table_r_ref.other_ref, f32[512,256]{1,0:T(8,128)} %pad_maximum_fusion.3.back_ref), custom_call_target="tpu_custom_call" | custom-call | bytes 90000000 | tf_op jit(solution)/shard_map/spread_rows/pallas_call | solution.py:259
  316.5 3.0 reduce_sum.62
  319.5 74.1 %all_to_all.43 = bf16[128,80,256]{2,1,0:T(8,128)(2,1)} all-to-all(bf16[128,80,256]{2,1,0:T(8,128)(2,1)} %bitcast.52), channel_id=1, replica_groups=mesh['grp'=4,'z'=4,'x'=4,'core'=2] {'grp','z','x','core'}, dimensions={0} | all-to-all | bytes 10485760 | tf_op jit(solution)/shard_map/all_to_all | solution.py:76
  393.6 4.4 all-to-all-start.6
  398.0 21.6 %absorb_rows.1 = f32[8192,256]{1,0:T(8,128)} custom-call(s32[10240]{0:T(1024)} %mul.348.place_ref, bf16[10240,256]{1,0:T(8,128)(2,1)} %bitcast.53), custom_call_target="tpu_custom_call" | custom-call | bytes 79200000 | tf_op jit(solution)/shard_map/absorb_rows/pallas_call | solution.py:314
  419.7 5.9 %all-to-all-done.6 = bf16[128,24,256]{2,1,0:T(8,128)(2,1)S(1)} async-done(((bf16[128,24,256]{2,1,0:T(8,128)(2,1)}), bf16[128,24,256]{2,1,0:T(8,128)(2,1)S(1)}, u32[]{:S(2)}, u32[]{:S(2)}) %all-to-all-start.6) | async-done | bytes 1572896 | tf_op jit(solution)/shard_map/all_to_all | solution.py:76
  425.6 21.6 %all-gather.5.cloned.1.call-done = bf16[1024,3072]{1,0:T(8,128)(2,1)} async-done(((bf16[8,3072]{1,0:T(8,128)(2,1)}), bf16[1024,3072]{1,0:T(8,128)(2,1)}) %all-gather.5.cloned.1.call-update) | async-done | bytes 6291472 | tf_op jit(solution)/shard_map/all_gather | solution.py:95
  447.1 4.7 %fusion.64 = (bf16[1024,1024]{1,0:T(8,128)(2,1)}, bf16[1024,1024]{1,0:T(8,128)(2,1)}) fusion(bf16[1024,3072]{1,0:T(8,128)(2,1)} %all-gather.5.cloned.1.call-done), kind=kLoop, calls=%fused_computation.118 | loop fusion | bytes 8388608 | tf_op jit(solution)/shard_map/split | solution.py:427
  451.8 2.8 fusion.63
  454.6 1.0 copy.71
  455.6 1.0 copy.72
  456.6 2.5 fusion.15
  (136 shorter events, 13.6 us)
Async XLA Ops:
  7.2 151.2 %copy-start = (bf16[1024,1024]{1,0:T(8,128)(2,1)S(1)}, bf16[1024,1024]{1,0:T(8,128)(2,1)}, u32[]{:S(2)}) copy-start(bf16[1024,1024]{1,0:T(8,128)(2,1)} %param.25) | copy-start | bytes 6291460
  33.1 30.1 %all-to-all-start.1 = ((bf16[128,24,256]{2,1,0:T(8,128)(2,1)}), bf16[128,24,256]{2,1,0:T(8,128)(2,1)}, u32[]{:S(2)}, u32[]{:S(2)}) async-start(bf16[128,24,256]{2,1,0:T(8,128)(2,1)} %bitcast.54), calls=%async_computation.1 | async-start | bytes 3145728 | tf_op jit(solution)/shard_map/all_to_all | solution.py:76
  63.2 5.7 %copy-start.25 = (s32[256,16]{0,1:T(8,128)S(1)}, s32[256,16]{0,1:T(8,128)}, u32[]{:S(2)}) copy-start(s32[256,16]{0,1:T(8,128)} %param.19) | copy-start | bytes 49156
  63.2 5.9 %copy-start.26 = (s32[256,16]{0,1:T(8,128)S(1)}, s32[256,16]{0,1:T(8,128)}, u32[]{:S(2)}) copy-start(s32[256,16]{0,1:T(8,128)} %param.21) | copy-start | bytes 49156
  63.2 6.1 %copy-start.27 = (s32[256,16]{0,1:T(8,128)S(1)}, s32[256,16]{0,1:T(8,128)}, u32[]{:S(2)}) copy-start(s32[256,16]{0,1:T(8,128)} %param.20) | copy-start | bytes 49156
  63.2 6.3 %copy-start.28 = (s32[256,16]{0,1:T(8,128)S(1)}, s32[256,16]{0,1:T(8,128)}, u32[]{:S(2)}) copy-start(s32[256,16]{0,1:T(8,128)} %param.22) | copy-start | bytes 49156
  63.2 69.7 %all-to-all-start.2 = ((bf16[128,80,256]{2,1,0:T(8,128)(2,1)}), bf16[128,80,256]{2,1,0:T(8,128)(2,1)}, u32[]{:S(2)}, u32[]{:S(2)}) async-start(bf16[128,80,256]{2,1,0:T(8,128)(2,1)} %bitcast.51), calls=%async_computation.2 | async-start | bytes 10485760 | tf_op jit(solution)/shard_map/all_to_all | solution.py:76
  68.8 150.9 %all-gather.3.cloned.1.call-start = ((), (), s32[]{:S(2)}) async-start(), calls=%async_computation.7 | async-start | bytes 8650752 | tf_op jit(solution)/shard_map/all_gather | solution.py:72
  132.9 18.8 %copy-start.9 = (bf16[256,1024]{1,0:T(8,128)(2,1)S(1)}, bf16[256,1024]{1,0:T(8,128)(2,1)}, u32[]{:S(2)}) copy-start(bf16[256,1024]{1,0:T(8,128)(2,1)} %param.27) | copy-start | bytes 1572868
  151.7 4.7 %copy-start.38 = (bf16[1024,256]{1,0:T(8,128)(2,1)S(1)}, bf16[1024,256]{1,0:T(8,128)(2,1)}, u32[]{:S(2)}) copy-start(bf16[1024,256]{1,0:T(8,128)(2,1)} %param.29) | copy-start | bytes 1572868
  153.9 4.1 copy-start.6
  153.9 4.1 copy-start.8
  157.1 3.4 copy-start.15
  158.0 2.5 copy-start.30
  158.3 1.5 copy-start.21
  159.2 1.4 copy-start.42
  219.8 4.6 copy-start.7
  219.8 4.6 copy-start.18
  219.8 4.6 copy-start.34
  224.4 2.0 copy-start.31
  224.4 2.0 copy-start.32
  224.4 2.1 copy-start.37
  224.4 2.1 copy-start.43
  226.5 1.7 copy-start.23
  226.5 1.7 copy-start.33
  228.9 12.9 %all-to-all-start.3 = ((f32[32,2,256]{2,1,0:T(2,128)}), f32[32,2,256]{2,1,0:T(2,128)S(1)}, u32[]{:S(2)}, u32[]{:S(2)}) async-start(f32[32,2,256]{2,1,0:T(2,128)} %broadcast_in_dim.2), calls=%async_computation.3 | async-start | bytes 131072 | tf_op jit(solution)/shard_map/all_to_all | solution.py:389
  241.8 6.7 %copy-start.16 = (f32[256,256]{0,1:T(8,128)S(1)}, f32[256,256]{0,1:T(8,128)}, u32[]{:S(2)}) copy-start(f32[256,256]{0,1:T(8,128)} %copy-done.15) | copy-start | bytes 786436
  241.9 6.7 %copy-start.29 = (f32[256]{0:T(256)S(1)}, f32[256]{0:T(256)}, u32[]{:S(2)}) copy-start(f32[256]{0:T(256)} %get-tuple-element.77) | copy-start | bytes 3076
  241.9 6.8 %copy-start.39 = (bf16[1024,256]{1,0:T(8,128)(2,1)S(1)}, bf16[1024,256]{1,0:T(8,128)(2,1)}, u32[]{:S(2)}) copy-start(bf16[1024,256]{1,0:T(8,128)(2,1)} %param.29) | copy-start | bytes 1572868
  248.6 2.3 copy-start.41
  248.7 2.9 copy-start.20
  250.9 1.6 copy-start.35
  253.9 4.5 copy-start.12
  253.9 1.5 copy-start.44
  253.9 2.1 copy-start.10
  256.6 2.4 copy-start.2
  258.0 4.9 %collective-permute-start = (bf16[512,1536]{1,0:T(8,128)(2,1)}, bf16[512,1536]{1,0:T(8,128)(2,1)}, u32[]{:S(2)}, u32[]{:S(2)}) collective-permute-start(bf16[512,1536]{1,0:T(8,128)(2,1)} %constant_dynamic-slice_fusion.1), channel_id=1, source_target_pairs={{0,1},{1,0},{2,3},{3,2},{4,5},{5,4},{6,7},{7,6},{8,9},{9,8},{10,11... | collective-permute-start | bytes 4718600 | tf_op jit(solution)/shard_map/ppermute | solution.py:83
  259.0 2.2 copy-start.4
  259.0 2.3 copy-start.11
  259.0 2.6 copy-start.13
  261.2 4.0 collective-permute-start.1
  261.3 2.1 copy-start.3
  262.0 3.2 copy-start.5
  269.1 47.4 %all-to-all-start.4 = ((bf16[64,8,3072]{2,1,0:T(8,128)(2,1)}), bf16[64,8,3072]{2,1,0:T(8,128)(2,1)}, u32[]{:S(2)}, u32[]{:S(2)}) async-start(bf16[64,8,3072]{2,1,0:T(8,128)(2,1)} %pad_maximum_fusion.2), calls=%async_computation.4 | async-start | bytes 6291456 | tf_op jit(solution)/shard_map/all_to_all | solution.py:90
  275.7 171.4 %all-gather.5.cloned.1.call-start = ((), (), s32[]{:S(2)}) async-start(), calls=%async_computation.8 | async-start | bytes 6340608 | tf_op jit(solution)/shard_map/all_gather | solution.py:95
  393.6 31.9 %all-to-all-start.6 = ((bf16[128,24,256]{2,1,0:T(8,128)(2,1)}), bf16[128,24,256]{2,1,0:T(8,128)(2,1)S(1)}, u32[]{:S(2)}, u32[]{:S(2)}) async-start(bf16[128,24,256]{2,1,0:T(8,128)(2,1)} %bitcast.16), calls=%async_computation.6 | async-start | bytes 3145728 | tf_op jit(solution)/shard_map/all_to_all | solution.py:76
  425.5 21.6 %copy-start.14 = (bf16[128,24,256]{2,1,0:T(8,128)(2,1)}, bf16[128,24,256]{2,1,0:T(8,128)(2,1)S(1)}, u32[]{:S(2)}) copy-start(bf16[128,24,256]{2,1,0:T(8,128)(2,1)S(1)} %all-to-all-done.6) | copy-start | bytes 4718596
  451.8 7.3 %copy-start.1 = (bf16[1024,1024]{1,0:T(8,128)(2,1)S(1)}, bf16[1024,1024]{1,0:T(8,128)(2,1)}, u32[]{:S(2)}) copy-start(bf16[1024,1024]{1,0:T(8,128)(2,1)} %param.25) | copy-start | bytes 6291460
  (7 other events, 7.5 us)
Sparse Core Ops, SparseCore 0:
  161.4 58.2 all-gather.2
  319.6 127.4 all-gather.4

commit v2 on v1

--- a/solution.py
+++ b/solution.py
@@ -412,15 +412,17 @@
     back_all, terms = lax.optimization_barrier((back_all, terms))
     part = chip_sum(terms)
     sums_q = spread_rows(slots_q, slots_r, table_r, back_all, table_q.shape[0], 25)
+    sums_q, back_all, part = lax.optimization_barrier((sums_q, back_all, part))
+    summed = gather_rows(part)
     sums_r = spread_rows(slots_r, slots_q, table_q, back_all, table_r.shape[0], 25)
-    sums_q, sums_r, part = lax.optimization_barrier((sums_q, sums_r, part))
-    summed = gather_rows(part)
+    sums_q, sums_r = lax.optimization_barrier((sums_q, sums_r))
     back_q = exchange(sums_q.reshape(lists, -1, features)).reshape(-1, features)
     back_q, sums_r = lax.optimization_barrier((back_q, sums_r))
     back_r = exchange(sums_r.reshape(lists, -1, features)).reshape(-1, features)
     grad_quotient = absorb_rows(asked_q, back_q, quotient.shape[0])
-    grad_quotient, back_r, summed = lax.optimization_barrier((grad_quotient, back_r, summed))
+    grad_quotient, back_r = lax.optimization_barrier((grad_quotient, back_r))
     grad_remainder = inner(named_r, back_r)
+    grad_remainder, summed = lax.optimization_barrier((grad_remainder, summed))
     hidden = query_w2.shape[0]
     weights_out = []
     for both in jnp.split(summed, 2, axis=1):

time: 467 us -> 468 us (level)
    all_gather x1, waiting for transfers between devices: 21.6 us -> 0.01 us  [gather_rows(): return lax.all_gather(part, ('core', *CHIP_AXES), axis=0, tiled=True)]
    all_to_all x1, waiting for transfers between devices: 0.33 us -> 18.4 us  [chip_sum(): lax.all_to_all(terms, CHIP_AXES, split_axis=0, concat_axis=0, tiled=True)]
    all_to_all x3, waiting for transfers between devices: 77.6 us -> 83.5 us  [exchange(): lax.all_to_all(rows, MESH_AXES, split_axis=0, concat_axis=0, tiled=True)]
  transfers between devices with their start and end apart: 9 -> 9, of which waited for: 7 -> 6; matrix products, arithmetic and copies ran while one was open for 3% -> 3% of each run, Pallas kernels for 17% -> 16%
where the time goes in v2:
time: 468 us; the launch traced here: 466 us
  waiting for transfers between devices  162 us (35%)
  Pallas kernels  95.7 us (20%)
  blocking collectives  94.5 us (20%)
  matrix products  36 us (8%)
  starting transfers between devices  28.1 us (6%)
  local copies, waits for them, and re-layouts  20.3 us (4%)
  between operations  14.7 us (3%)
  other arithmetic  14.6 us (3%)
    all_to_all x2, blocking collectives, exchange(): lax.all_to_all(rows, MESH_AXES, split_axis=0, concat_axis=0, tiled=True)  94.5 us
    all_to_all x3, waiting for transfers between devices, exchange(): lax.all_to_all(rows, MESH_AXES, split_axis=0, concat_axis=0, tiled=True)  83.5 us
    all_gather x1, waiting for transfers between devices, gather_group(): return lax.all_gather(values, GROUP_AXES, axis=0, tiled=True)  56.6 us
    pallas_call x2, Pallas kernels, spread_rows(): pl.pallas_call(spread_kernel, out_shape=jax.ShapeDtypeStruct((rows, featu...  40.4 us
    pallas_call x1, Pallas kernels, absorb_rows(): pl.pallas_call(functools.partial(absorb_kernel, steps, batch, unroll), gr...  21.6 us
    pallas_call x1, Pallas kernels, pool_rows(): pl.pallas_call(pool_kernel, out_shape=jax.ShapeDtypeStruct((examples, fea...  18.8 us
    all_to_all x1, waiting for transfers between devices, chip_sum(): lax.all_to_all(terms, CHIP_AXES, split_axis=0, concat_axis=0, tiled=True)  18.4 us
    all_to_all x3, starting transfers between devices, exchange(): lax.all_to_all(rows, MESH_AXES, split_axis=0, concat_axis=0, tiled=True)  15.3 us
  transfers between devices with their start and end apart: 9, of which 6 were waited for; matrix products, arithmetic and copies ran while one was open for 3% of the time, Pallas kernels for 16%

profile of v2, /device:TPU:1, one launch (start us, length us, event | category | flops | bytes accessed | tf_op | source)
XLA Modules:
  0.0 466.4 jit_solution(17973876787115981970)
XLA Ops:
  7.2 1.0 copy.59
  8.2 0.8 copy.60
  9.1 20.8 %all_to_all.42 = s32[128,1,104]{2,1,0:T(1,128)S(1)} all-to-all(s32[128,1,104]{2,1,0:T(1,128)S(1)} %bitcast.58), channel_id=1, replica_groups=mesh['grp'=4,'z'=4,'x'=4,'core'=2] {'grp','z','x','core'}, dimensions={0} | all-to-all | bytes 106496 | tf_op jit(solution)/shard_map/all_to_all | solution.py:76
  30.1 3.1 convolution_convert_fusion
  33.1 5.3 %all-to-all-start.1 = ((bf16[128,24,256]{2,1,0:T(8,128)(2,1)}), bf16[128,24,256]{2,1,0:T(8,128)(2,1)}, u32[]{:S(2)}, u32[]{:S(2)}) async-start(bf16[128,24,256]{2,1,0:T(8,128)(2,1)} %bitcast.54), calls=%async_computation.1 | async-start | bytes 3145728 | tf_op jit(solution)/shard_map/all_to_all | solution.py:76
  39.2 14.8 %pick_rows.1 = bf16[10240,256]{1,0:T(8,128)(2,1)} custom-call(s32[10240]{0:T(1024)} %mul.348.place_ref, bf16[8192,256]{1,0:T(8,128)(2,1)} %table_ref.1), custom_call_target="tpu_custom_call" | custom-call | bytes 43200000 | tf_op jit(solution)/shard_map/pick_rows/pallas_call | solution.py:170
  54.0 9.2 %all-to-all-done.1 = bf16[128,24,256]{2,1,0:T(8,128)(2,1)} async-done(((bf16[128,24,256]{2,1,0:T(8,128)(2,1)}), bf16[128,24,256]{2,1,0:T(8,128)(2,1)}, u32[]{:S(2)}, u32[]{:S(2)}) %all-to-all-start.1) | async-done | bytes 1572896 | tf_op jit(solution)/shard_map/all_to_all | solution.py:76
  63.2 5.6 %all-to-all-start.2 = ((bf16[128,80,256]{2,1,0:T(8,128)(2,1)}), bf16[128,80,256]{2,1,0:T(8,128)(2,1)}, u32[]{:S(2)}, u32[]{:S(2)}) async-start(bf16[128,80,256]{2,1,0:T(8,128)(2,1)} %bitcast.51), calls=%async_computation.2 | async-start | bytes 10485760 | tf_op jit(solution)/shard_map/all_to_all | solution.py:76
  70.4 62.5 %all-to-all-done.2 = bf16[128,80,256]{2,1,0:T(8,128)(2,1)} async-done(((bf16[128,80,256]{2,1,0:T(8,128)(2,1)}), bf16[128,80,256]{2,1,0:T(8,128)(2,1)}, u32[]{:S(2)}, u32[]{:S(2)}) %all-to-all-start.2) | async-done | bytes 5242912 | tf_op jit(solution)/shard_map/all_to_all | solution.py:76
  132.9 18.8 %pool_rows.1 = bf16[512,256]{1,0:T(8,128)(2,1)} custom-call(s32[8192]{0:T(1024)} %get-tuple-element.98.place_q_ref.place_ref.other_place_ref, s32[8192]{0:T(1024)} %get-tuple-element.99.place_r_ref.other_place_ref.place_ref, bf16[10240,256]{1,0:T(8,128)(2,1)} %bitcast.7.table_q_ref.other_ref, bf16[3072,256]{1,0:T(8,128)(2,1)} %bitcast.5.table_r_ref.other_ref), custom_call_target="tpu_custom_call" | custom-call | bytes 64800000 | tf_op jit(solution)/shard_map/pool_rows/pallas_call | solution.py:210
  151.7 1.3 fusion.51
  153.0 1.0 copy-done.18
  153.9 2.5 fusion.60
  158.3 0.8 fusion.59
  161.3 1.3 convert_element_type.113
  163.1 56.6 %all-gather.3.cloned.1.call-done = bf16[8192,512]{0,1:T(8,128)(2,1)} async-done(((bf16[256,512]{0,1:T(8,128)(2,1)}), bf16[8192,512]{0,1:T(8,128)(2,1)}) %all-gather.3.cloned.1.call-update) | async-done | bytes 8388624 | tf_op jit(solution)/shard_map/all_gather | solution.py:72
  219.7 4.1 fusion.66
  224.4 2.0 multiply_reduce_fusion.1
  226.5 1.7 fusion.33
  228.8 5.6 %all-to-all-start.3 = ((f32[32,2,256]{2,1,0:T(2,128)}), f32[32,2,256]{2,1,0:T(2,128)S(1)}, u32[]{:S(2)}, u32[]{:S(2)}) async-start(f32[32,2,256]{2,1,0:T(2,128)} %broadcast_in_dim.2), calls=%async_computation.3 | async-start | bytes 131072 | tf_op jit(solution)/shard_map/all_to_all | solution.py:389
  234.4 3.4 fusion.26
  237.9 3.9 all-to-all-done.3
  241.8 6.7 %multiply_reduce_fusion = (f32[256]{0:T(256)S(1)}, f32[256,256]{0,1:T(8,128)S(1)}) fusion(f32[256,256]{0,1:T(8,128)} %copy-done.14, bf16[8192,512]{0,1:T(8,128)(2,1)} %all-gather.3.cloned.1.call-done, f32[8192]{0:T(1024)S(1)} %bitcast.62, f32[8192]{0:T(1024)S(1)} %bitcast.61, f32[256]{0:T(256)} %add_convert_fusion.2, f32[256]{0:T(256)} %copy-done.29), kind=kOutput, calls=%fused_computation.82 | convolution fusion | flops 2162491136 | bytes 9243648 | tf_op jit(solution)/shard_map/dot_general | solution.py:403
  248.6 2.2 fusion.47
  251.5 0.9 convolution_convert_fusion.1
  252.5 1.3 fusion.40
  253.8 0.9 convolution_convert_fusion.2
  256.5 1.4 constant_dynamic-slice_fusion.1
  259.0 1.3 constant_dynamic-slice_fusion
  260.2 0.9 copy-done.4
  262.0 0.8 pad_maximum_fusion.3.back_ref
  263.3 1.8 fusion.16
  265.1 1.8 fusion.17
  266.9 2.1 pad_maximum_fusion.2
  269.0 6.6 %all-to-all-start.4 = ((bf16[64,8,3072]{2,1,0:T(8,128)(2,1)}), bf16[64,8,3072]{2,1,0:T(8,128)(2,1)}, u32[]{:S(2)}, u32[]{:S(2)}) async-start(bf16[64,8,3072]{2,1,0:T(8,128)(2,1)} %pad_maximum_fusion.2), calls=%async_computation.4 | async-start | bytes 6291456 | tf_op jit(solution)/shard_map/all_to_all | solution.py:90
  275.7 22.0 %spread_rows.2 = bf16[10240,256]{1,0:T(8,128)(2,1)} custom-call(s32[8192]{0:T(1024)} %get-tuple-element.98.place_q_ref.place_ref.other_place_ref, s32[8192]{0:T(1024)} %get-tuple-element.99.place_r_ref.other_place_ref.place_ref, bf16[3072,256]{1,0:T(8,128)(2,1)} %bitcast.5.table_r_ref.other_ref, f32[512,256]{1,0:T(8,128)} %pad_maximum_fusion.3.back_ref), custom_call_target="tpu_custom_call" | custom-call | bytes 90000000 | tf_op jit(solution)/shard_map/spread_rows/pallas_call | solution.py:259
  297.7 18.4 %all-to-all-done.4 = bf16[64,8,3072]{2,1,0:T(8,128)(2,1)} async-done(((bf16[64,8,3072]{2,1,0:T(8,128)(2,1)}), bf16[64,8,3072]{2,1,0:T(8,128)(2,1)}, u32[]{:S(2)}, u32[]{:S(2)}) %all-to-all-start.4) | async-done | bytes 3145760 | tf_op jit(solution)/shard_map/all_to_all | solution.py:90
  316.1 3.0 reduce_sum.62
  319.1 18.4 %spread_rows.3 = bf16[3072,256]{1,0:T(8,128)(2,1)} custom-call(s32[8192]{0:T(1024)} %get-tuple-element.99.place_r_ref.other_place_ref.place_ref, s32[8192]{0:T(1024)} %get-tuple-element.98.place_q_ref.place_ref.other_place_ref, bf16[10240,256]{1,0:T(8,128)(2,1)} %bitcast.7.table_q_ref.other_ref, f32[512,256]{1,0:T(8,128)} %pad_maximum_fusion.3.back_ref), custom_call_target="tpu_custom_call" | custom-call | bytes 90000000 | tf_op jit(solution)/shard_map/spread_rows/pallas_call | solution.py:259
  337.6 73.7 %all_to_all.43 = bf16[128,80,256]{2,1,0:T(8,128)(2,1)} all-to-all(bf16[128,80,256]{2,1,0:T(8,128)(2,1)} %bitcast.52), channel_id=1, replica_groups=mesh['grp'=4,'z'=4,'x'=4,'core'=2] {'grp','z','x','core'}, dimensions={0} | all-to-all | bytes 10485760 | tf_op jit(solution)/shard_map/all_to_all | solution.py:76
  411.2 4.4 all-to-all-start.6
  415.6 21.6 %absorb_rows.1 = f32[8192,256]{1,0:T(8,128)} custom-call(s32[10240]{0:T(1024)} %mul.348.place_ref, bf16[10240,256]{1,0:T(8,128)(2,1)} %bitcast.53), custom_call_target="tpu_custom_call" | custom-call | bytes 79200000 | tf_op jit(solution)/shard_map/absorb_rows/pallas_call | solution.py:314
  437.3 11.7 %all-to-all-done.6 = bf16[128,24,256]{2,1,0:T(8,128)(2,1)S(1)} async-done(((bf16[128,24,256]{2,1,0:T(8,128)(2,1)}), bf16[128,24,256]{2,1,0:T(8,128)(2,1)S(1)}, u32[]{:S(2)}, u32[]{:S(2)}) %all-to-all-start.6) | async-done | bytes 1572896 | tf_op jit(solution)/shard_map/all_to_all | solution.py:76
  449.0 1.1 fusion.15
  450.1 4.8 %fusion.64 = (bf16[1024,1024]{1,0:T(8,128)(2,1)}, bf16[1024,1024]{1,0:T(8,128)(2,1)}) fusion(bf16[1024,3072]{1,0:T(8,128)(2,1)} %all-gather.5.cloned.1.call-done), kind=kLoop, calls=%fused_computation.118 | loop fusion | bytes 8388608 | tf_op jit(solution)/shard_map/split | solution.py:429
  455.0 2.6 fusion.63
  457.6 1.0 copy.71
  458.6 1.0 copy.72
  (134 shorter events, 13.2 us)
Async XLA Ops:
  7.2 151.1 %copy-start = (bf16[1024,1024]{1,0:T(8,128)(2,1)S(1)}, bf16[1024,1024]{1,0:T(8,128)(2,1)}, u32[]{:S(2)}) copy-start(bf16[1024,1024]{1,0:T(8,128)(2,1)} %param.25) | copy-start | bytes 6291460
  33.1 30.1 %all-to-all-start.1 = ((bf16[128,24,256]{2,1,0:T(8,128)(2,1)}), bf16[128,24,256]{2,1,0:T(8,128)(2,1)}, u32[]{:S(2)}, u32[]{:S(2)}) async-start(bf16[128,24,256]{2,1,0:T(8,128)(2,1)} %bitcast.54), calls=%async_computation.1 | async-start | bytes 3145728 | tf_op jit(solution)/shard_map/all_to_all | solution.py:76
  63.2 5.7 %copy-start.24 = (s32[256,16]{0,1:T(8,128)S(1)}, s32[256,16]{0,1:T(8,128)}, u32[]{:S(2)}) copy-start(s32[256,16]{0,1:T(8,128)} %param.19) | copy-start | bytes 49156
  63.2 5.9 %copy-start.25 = (s32[256,16]{0,1:T(8,128)S(1)}, s32[256,16]{0,1:T(8,128)}, u32[]{:S(2)}) copy-start(s32[256,16]{0,1:T(8,128)} %param.21) | copy-start | bytes 49156
  63.2 6.1 %copy-start.26 = (s32[256,16]{0,1:T(8,128)S(1)}, s32[256,16]{0,1:T(8,128)}, u32[]{:S(2)}) copy-start(s32[256,16]{0,1:T(8,128)} %param.20) | copy-start | bytes 49156
  63.2 6.3 %copy-start.27 = (s32[256,16]{0,1:T(8,128)S(1)}, s32[256,16]{0,1:T(8,128)}, u32[]{:S(2)}) copy-start(s32[256,16]{0,1:T(8,128)} %param.22) | copy-start | bytes 49156
  63.2 69.7 %all-to-all-start.2 = ((bf16[128,80,256]{2,1,0:T(8,128)(2,1)}), bf16[128,80,256]{2,1,0:T(8,128)(2,1)}, u32[]{:S(2)}, u32[]{:S(2)}) async-start(bf16[128,80,256]{2,1,0:T(8,128)(2,1)} %bitcast.51), calls=%async_computation.2 | async-start | bytes 10485760 | tf_op jit(solution)/shard_map/all_to_all | solution.py:76
  68.8 150.9 %all-gather.3.cloned.1.call-start = ((), (), s32[]{:S(2)}) async-start(), calls=%async_computation.7 | async-start | bytes 8650752 | tf_op jit(solution)/shard_map/all_gather | solution.py:72
  132.9 18.8 %copy-start.9 = (bf16[256,1024]{1,0:T(8,128)(2,1)S(1)}, bf16[256,1024]{1,0:T(8,128)(2,1)}, u32[]{:S(2)}) copy-start(bf16[256,1024]{1,0:T(8,128)(2,1)} %param.27) | copy-start | bytes 1572868
  151.7 4.7 %copy-start.37 = (bf16[1024,256]{1,0:T(8,128)(2,1)S(1)}, bf16[1024,256]{1,0:T(8,128)(2,1)}, u32[]{:S(2)}) copy-start(bf16[1024,256]{1,0:T(8,128)(2,1)} %param.29) | copy-start | bytes 1572868
  153.9 4.0 copy-start.6
  153.9 4.0 copy-start.8
  157.1 3.4 copy-start.14
  158.0 2.5 copy-start.29
  158.3 1.5 copy-start.20
  159.1 1.4 copy-start.41
  219.7 4.6 copy-start.7
  219.7 4.6 copy-start.17
  219.7 4.6 copy-start.33
  224.4 2.0 copy-start.30
  224.4 2.0 copy-start.31
  224.4 2.1 copy-start.36
  224.4 2.1 copy-start.42
  226.5 1.7 copy-start.22
  226.5 1.7 copy-start.32
  228.8 12.9 %all-to-all-start.3 = ((f32[32,2,256]{2,1,0:T(2,128)}), f32[32,2,256]{2,1,0:T(2,128)S(1)}, u32[]{:S(2)}, u32[]{:S(2)}) async-start(f32[32,2,256]{2,1,0:T(2,128)} %broadcast_in_dim.2), calls=%async_computation.3 | async-start | bytes 131072 | tf_op jit(solution)/shard_map/all_to_all | solution.py:389
  241.8 6.7 %copy-start.15 = (f32[256,256]{0,1:T(8,128)S(1)}, f32[256,256]{0,1:T(8,128)}, u32[]{:S(2)}) copy-start(f32[256,256]{0,1:T(8,128)} %copy-done.14) | copy-start | bytes 786436
  241.8 6.7 %copy-start.28 = (f32[256]{0:T(256)S(1)}, f32[256]{0:T(256)}, u32[]{:S(2)}) copy-start(f32[256]{0:T(256)} %get-tuple-element.83) | copy-start | bytes 3076
  241.8 6.8 %copy-start.38 = (bf16[1024,256]{1,0:T(8,128)(2,1)S(1)}, bf16[1024,256]{1,0:T(8,128)(2,1)}, u32[]{:S(2)}) copy-start(bf16[1024,256]{1,0:T(8,128)(2,1)} %param.29) | copy-start | bytes 1572868
  248.6 2.3 copy-start.40
  248.6 2.9 copy-start.19
  250.9 1.6 copy-start.34
  252.5 1.4 copy-start.44
  253.8 4.5 copy-start.12
  253.8 1.5 copy-start.43
  253.8 2.1 copy-start.10
  256.5 2.4 copy-start.2
  257.9 4.9 %collective-permute-start = (bf16[512,1536]{1,0:T(8,128)(2,1)}, bf16[512,1536]{1,0:T(8,128)(2,1)}, u32[]{:S(2)}, u32[]{:S(2)}) collective-permute-start(bf16[512,1536]{1,0:T(8,128)(2,1)} %constant_dynamic-slice_fusion.1), channel_id=1, source_target_pairs={{0,1},{1,0},{2,3},{3,2},{4,5},{5,4},{6,7},{7,6},{8,9},{9,8},{10,11... | collective-permute-start | bytes 4718600 | tf_op jit(solution)/shard_map/ppermute | solution.py:83
  258.9 2.2 copy-start.4
  259.0 2.3 copy-start.11
  259.0 2.6 copy-start.13
  261.1 4.0 collective-permute-start.1
  261.2 2.1 copy-start.3
  262.0 3.2 copy-start.5
  269.0 47.1 %all-to-all-start.4 = ((bf16[64,8,3072]{2,1,0:T(8,128)(2,1)}), bf16[64,8,3072]{2,1,0:T(8,128)(2,1)}, u32[]{:S(2)}, u32[]{:S(2)}) async-start(bf16[64,8,3072]{2,1,0:T(8,128)(2,1)} %pad_maximum_fusion.2), calls=%async_computation.4 | async-start | bytes 6291456 | tf_op jit(solution)/shard_map/all_to_all | solution.py:90
  275.6 174.5 %all-gather.5.cloned.1.call-start = ((), (), s32[]{:S(2)}) async-start(), calls=%async_computation.8 | async-start | bytes 6340608 | tf_op jit(solution)/shard_map/all_gather | solution.py:95
  411.2 37.8 %all-to-all-start.6 = ((bf16[128,24,256]{2,1,0:T(8,128)(2,1)}), bf16[128,24,256]{2,1,0:T(8,128)(2,1)S(1)}, u32[]{:S(2)}, u32[]{:S(2)}) async-start(bf16[128,24,256]{2,1,0:T(8,128)(2,1)} %bitcast.16), calls=%async_computation.6 | async-start | bytes 3145728 | tf_op jit(solution)/shard_map/all_to_all | solution.py:76
  450.1 9.5 %copy-start.1 = (bf16[1024,1024]{1,0:T(8,128)(2,1)S(1)}, bf16[1024,1024]{1,0:T(8,128)(2,1)}, u32[]{:S(2)}) copy-start(bf16[1024,1024]{1,0:T(8,128)(2,1)} %param.25) | copy-start | bytes 6291460
  (6 other events, 6.1 us)
Sparse Core Ops, SparseCore 0:
  161.4 58.2 all-gather.2
  319.2 126.5 all-gather.4

commit v3 on v1

--- a/solution.py
+++ b/solution.py
@@ -192,14 +192,13 @@
 
     def body(first):
         for j in range(group):
-            bag_at = pl.ds((first + j) * bag, bag)
-            places_q, places_r = place_q_ref.at[bag_at], place_r_ref.at[bag_at]
-            terms = [
-                wide_q[row(places_q[l]), :] * wide_r[row(places_r[l]), :] for l in range(bag)
-            ]
-            while len(terms) > 1:
-                terms = [a + b for a, b in zip(terms[::2], terms[1::2], strict=True)]
-            stage_ref[pl.ds(2 * j, 2), :] = terms[0]
+            place = (first + j) * bag
+            total = None
+            for l in range(bag):
+                left = wide_q[row(place_q_ref[place + l]), :]
+                term = left * wide_r[row(place_r_ref[place + l]), :]
+                total = term if total is None else total + term
+            stage_ref[pl.ds(2 * j, 2), :] = total
         out_ref[pl.ds(first, group), :] = joined(stage_ref, 0, group).astype(jnp.bfloat16)
 
     loop(examples, group, body)
@@ -419,8 +418,9 @@
     back_q, sums_r = lax.optimization_barrier((back_q, sums_r))
     back_r = exchange(sums_r.reshape(lists, -1, features)).reshape(-1, features)
     grad_quotient = absorb_rows(asked_q, back_q, quotient.shape[0])
-    grad_quotient, back_r, summed = lax.optimization_barrier((grad_quotient, back_r, summed))
+    grad_quotient, back_r = lax.optimization_barrier((grad_quotient, back_r))
     grad_remainder = inner(named_r, back_r)
+    grad_remainder, summed = lax.optimization_barrier((grad_remainder, summed))
     hidden = query_w2.shape[0]
     weights_out = []
     for both in jnp.split(summed, 2, axis=1):

time: 467 us -> 462 us (0.989)
  transfers between devices with their start and end apart: 9 -> 9, of which waited for: 7 -> 6; matrix products, arithmetic and copies ran while one was open for 3% -> 3% of each run, Pallas kernels for 17% -> 17%
where the time goes in v3:
time: 462 us; the launch traced here: 461 us
  waiting for transfers between devices  159 us (34%)
  blocking collectives  95.3 us (21%)
  Pallas kernels  93.3 us (20%)
  matrix products  36 us (8%)
  starting transfers between devices  28.1 us (6%)
  local copies, waits for them, and re-layouts  20.3 us (4%)
  between operations  14.7 us (3%)
  other arithmetic  14.6 us (3%)
    all_to_all x2, blocking collectives, exchange(): lax.all_to_all(rows, MESH_AXES, split_axis=0, concat_axis=0, tiled=True)  95.3 us
    all_to_all x3, waiting for transfers between devices, exchange(): lax.all_to_all(rows, MESH_AXES, split_axis=0, concat_axis=0, tiled=True)  77.6 us
    all_gather x1, waiting for transfers between devices, gather_group(): return lax.all_gather(values, GROUP_AXES, axis=0, tiled=True)  56.6 us
    pallas_call x2, Pallas kernels, spread_rows(): pl.pallas_call(spread_kernel, out_shape=jax.ShapeDtypeStruct((rows, featu...  40.4 us
    pallas_call x1, Pallas kernels, absorb_rows(): pl.pallas_call(functools.partial(absorb_kernel, steps, batch, unroll), gr...  21.6 us
    all_gather x1, waiting for transfers between devices, gather_rows(): return lax.all_gather(part, ('core', *CHIP_AXES), axis=0, tiled=True)  20.5 us
    pallas_call x1, Pallas kernels, pool_rows(): pl.pallas_call(pool_kernel, out_shape=jax.ShapeDtypeStruct((examples, fea...  16.3 us
    all_to_all x3, starting transfers between devices, exchange(): lax.all_to_all(rows, MESH_AXES, split_axis=0, concat_axis=0, tiled=True)  15.3 us
  transfers between devices with their start and end apart: 9, of which 6 were waited for; matrix products, arithmetic and copies ran while one was open for 3% of the time, Pallas kernels for 17%

profile of v3, /device:TPU:1, one launch (start us, length us, event | category | flops | bytes accessed | tf_op | source)
XLA Modules:
  0.0 460.9 jit_solution(6388337376608693694)
XLA Ops:
  7.2 1.0 copy.59
  8.2 0.8 copy.60
  9.1 20.8 %all_to_all.42 = s32[128,1,104]{2,1,0:T(1,128)S(1)} all-to-all(s32[128,1,104]{2,1,0:T(1,128)S(1)} %bitcast.58), channel_id=1, replica_groups=mesh['grp'=4,'z'=4,'x'=4,'core'=2] {'grp','z','x','core'}, dimensions={0} | all-to-all | bytes 106496 | tf_op jit(solution)/shard_map/all_to_all | solution.py:76
  30.1 3.1 convolution_convert_fusion
  33.1 5.3 %all-to-all-start.1 = ((bf16[128,24,256]{2,1,0:T(8,128)(2,1)}), bf16[128,24,256]{2,1,0:T(8,128)(2,1)}, u32[]{:S(2)}, u32[]{:S(2)}) async-start(bf16[128,24,256]{2,1,0:T(8,128)(2,1)} %bitcast.54), calls=%async_computation.1 | async-start | bytes 3145728 | tf_op jit(solution)/shard_map/all_to_all | solution.py:76
  39.2 14.9 %pick_rows.1 = bf16[10240,256]{1,0:T(8,128)(2,1)} custom-call(s32[10240]{0:T(1024)} %mul.348.place_ref, bf16[8192,256]{1,0:T(8,128)(2,1)} %table_ref.1), custom_call_target="tpu_custom_call" | custom-call | bytes 43200000 | tf_op jit(solution)/shard_map/pick_rows/pallas_call | solution.py:170
  54.1 9.2 %all-to-all-done.1 = bf16[128,24,256]{2,1,0:T(8,128)(2,1)} async-done(((bf16[128,24,256]{2,1,0:T(8,128)(2,1)}), bf16[128,24,256]{2,1,0:T(8,128)(2,1)}, u32[]{:S(2)}, u32[]{:S(2)}) %all-to-all-start.1) | async-done | bytes 1572896 | tf_op jit(solution)/shard_map/all_to_all | solution.py:76
  63.2 5.6 %all-to-all-start.2 = ((bf16[128,80,256]{2,1,0:T(8,128)(2,1)}), bf16[128,80,256]{2,1,0:T(8,128)(2,1)}, u32[]{:S(2)}, u32[]{:S(2)}) async-start(bf16[128,80,256]{2,1,0:T(8,128)(2,1)} %bitcast.51), calls=%async_computation.2 | async-start | bytes 10485760 | tf_op jit(solution)/shard_map/all_to_all | solution.py:76
  70.4 62.5 %all-to-all-done.2 = bf16[128,80,256]{2,1,0:T(8,128)(2,1)} async-done(((bf16[128,80,256]{2,1,0:T(8,128)(2,1)}), bf16[128,80,256]{2,1,0:T(8,128)(2,1)}, u32[]{:S(2)}, u32[]{:S(2)}) %all-to-all-start.2) | async-done | bytes 5242912 | tf_op jit(solution)/shard_map/all_to_all | solution.py:76
  132.9 16.3 %pool_rows.1 = bf16[512,256]{1,0:T(8,128)(2,1)} custom-call(s32[8192]{0:T(1024)} %get-tuple-element.94.place_q_ref.place_ref.other_place_ref, s32[8192]{0:T(1024)} %get-tuple-element.95.place_r_ref.other_place_ref.place_ref, bf16[10240,256]{1,0:T(8,128)(2,1)} %bitcast.7.table_q_ref.other_ref, bf16[3072,256]{1,0:T(8,128)(2,1)} %bitcast.5.table_r_ref.other_ref), custom_call_target="tpu_custom_call" | custom-call | bytes 64800000 | tf_op jit(solution)/shard_map/pool_rows/pallas_call | solution.py:209
  149.2 1.3 fusion.51
  150.5 1.0 copy-done.18
  151.5 2.5 fusion.60
  155.8 0.8 fusion.59
  158.8 1.3 convert_element_type.113
  160.6 56.6 %all-gather.3.cloned.1.call-done = bf16[8192,512]{0,1:T(8,128)(2,1)} async-done(((bf16[256,512]{0,1:T(8,128)(2,1)}), bf16[8192,512]{0,1:T(8,128)(2,1)}) %all-gather.3.cloned.1.call-update) | async-done | bytes 8388624 | tf_op jit(solution)/shard_map/all_gather | solution.py:72
  217.2 4.1 fusion.66
  221.9 2.0 multiply_reduce_fusion.1
  224.0 1.7 fusion.33
  226.3 5.6 %all-to-all-start.3 = ((f32[32,2,256]{2,1,0:T(2,128)}), f32[32,2,256]{2,1,0:T(2,128)S(1)}, u32[]{:S(2)}, u32[]{:S(2)}) async-start(f32[32,2,256]{2,1,0:T(2,128)} %broadcast_in_dim.2), calls=%async_computation.3 | async-start | bytes 131072 | tf_op jit(solution)/shard_map/all_to_all | solution.py:388
  231.9 3.4 fusion.26
  235.4 3.9 all-to-all-done.3
  239.4 6.7 %multiply_reduce_fusion = (f32[256]{0:T(256)S(1)}, f32[256,256]{0,1:T(8,128)S(1)}) fusion(f32[256,256]{0,1:T(8,128)} %copy-done.14, bf16[8192,512]{0,1:T(8,128)(2,1)} %all-gather.3.cloned.1.call-done, f32[8192]{0:T(1024)S(1)} %bitcast.62, f32[8192]{0:T(1024)S(1)} %bitcast.61, f32[256]{0:T(256)} %add_convert_fusion.2, f32[256]{0:T(256)} %copy-done.29), kind=kOutput, calls=%fused_computation.82 | convolution fusion | flops 2162491136 | bytes 9243648 | tf_op jit(solution)/shard_map/dot_general | solution.py:402
  246.1 2.2 fusion.47
  249.0 0.9 convolution_convert_fusion.1
  250.0 1.3 fusion.40
  251.3 0.9 convolution_convert_fusion.2
  254.1 1.4 constant_dynamic-slice_fusion.1
  256.5 1.3 constant_dynamic-slice_fusion
  257.8 0.9 copy-done.4
  259.5 0.8 pad_maximum_fusion.3.back_ref
  260.8 1.8 fusion.16
  262.7 1.8 fusion.17
  264.5 2.1 pad_maximum_fusion.2
  266.6 6.6 %all-to-all-start.4 = ((bf16[64,8,3072]{2,1,0:T(8,128)(2,1)}), bf16[64,8,3072]{2,1,0:T(8,128)(2,1)}, u32[]{:S(2)}, u32[]{:S(2)}) async-start(bf16[64,8,3072]{2,1,0:T(8,128)(2,1)} %pad_maximum_fusion.2), calls=%async_computation.4 | async-start | bytes 6291456 | tf_op jit(solution)/shard_map/all_to_all | solution.py:90
  273.2 18.4 %spread_rows.3 = bf16[3072,256]{1,0:T(8,128)(2,1)} custom-call(s32[8192]{0:T(1024)} %get-tuple-element.95.place_r_ref.other_place_ref.place_ref, s32[8192]{0:T(1024)} %get-tuple-element.94.place_q_ref.place_ref.other_place_ref, bf16[10240,256]{1,0:T(8,128)(2,1)} %bitcast.7.table_q_ref.other_ref, f32[512,256]{1,0:T(8,128)} %pad_maximum_fusion.3.back_ref), custom_call_target="tpu_custom_call" | custom-call | bytes 90000000 | tf_op jit(solution)/shard_map/spread_rows/pallas_call | solution.py:258
  291.7 22.0 %spread_rows.2 = bf16[10240,256]{1,0:T(8,128)(2,1)} custom-call(s32[8192]{0:T(1024)} %get-tuple-element.94.place_q_ref.place_ref.other_place_ref, s32[8192]{0:T(1024)} %get-tuple-element.95.place_r_ref.other_place_ref.place_ref, bf16[3072,256]{1,0:T(8,128)(2,1)} %bitcast.5.table_r_ref.other_ref, f32[512,256]{1,0:T(8,128)} %pad_maximum_fusion.3.back_ref), custom_call_target="tpu_custom_call" | custom-call | bytes 90000000 | tf_op jit(solution)/shard_map/spread_rows/pallas_call | solution.py:258
  313.6 3.0 reduce_sum.62
  316.6 74.5 %all_to_all.43 = bf16[128,80,256]{2,1,0:T(8,128)(2,1)} all-to-all(bf16[128,80,256]{2,1,0:T(8,128)(2,1)} %bitcast.52), channel_id=1, replica_groups=mesh['grp'=4,'z'=4,'x'=4,'core'=2] {'grp','z','x','core'}, dimensions={0} | all-to-all | bytes 10485760 | tf_op jit(solution)/shard_map/all_to_all | solution.py:76
  391.1 4.4 all-to-all-start.6
  395.5 21.6 %absorb_rows.1 = f32[8192,256]{1,0:T(8,128)} custom-call(s32[10240]{0:T(1024)} %mul.348.place_ref, bf16[10240,256]{1,0:T(8,128)(2,1)} %bitcast.53), custom_call_target="tpu_custom_call" | custom-call | bytes 79200000 | tf_op jit(solution)/shard_map/absorb_rows/pallas_call | solution.py:313
  417.1 5.9 %all-to-all-done.6 = bf16[128,24,256]{2,1,0:T(8,128)(2,1)S(1)} async-done(((bf16[128,24,256]{2,1,0:T(8,128)(2,1)}), bf16[128,24,256]{2,1,0:T(8,128)(2,1)S(1)}, u32[]{:S(2)}, u32[]{:S(2)}) %all-to-all-start.6) | async-done | bytes 1572896 | tf_op jit(solution)/shard_map/all_to_all | solution.py:76
  423.0 1.1 fusion.15
  424.1 20.5 %all-gather.5.cloned.1.call-done = bf16[1024,3072]{1,0:T(8,128)(2,1)} async-done(((bf16[8,3072]{1,0:T(8,128)(2,1)}), bf16[1024,3072]{1,0:T(8,128)(2,1)}) %all-gather.5.cloned.1.call-update) | async-done | bytes 6291472 | tf_op jit(solution)/shard_map/all_gather | solution.py:95
  444.6 4.8 %fusion.64 = (bf16[1024,1024]{1,0:T(8,128)(2,1)}, bf16[1024,1024]{1,0:T(8,128)(2,1)}) fusion(bf16[1024,3072]{1,0:T(8,128)(2,1)} %all-gather.5.cloned.1.call-done), kind=kLoop, calls=%fused_computation.118 | loop fusion | bytes 8388608 | tf_op jit(solution)/shard_map/split | solution.py:427
  449.4 2.6 fusion.63
  452.1 1.0 copy.71
  453.1 1.0 copy.72
  (134 shorter events, 13.2 us)
Async XLA Ops:
  7.2 148.6 %copy-start = (bf16[1024,1024]{1,0:T(8,128)(2,1)S(1)}, bf16[1024,1024]{1,0:T(8,128)(2,1)}, u32[]{:S(2)}) copy-start(bf16[1024,1024]{1,0:T(8,128)(2,1)} %param.25) | copy-start | bytes 6291460
  33.1 30.1 %all-to-all-start.1 = ((bf16[128,24,256]{2,1,0:T(8,128)(2,1)}), bf16[128,24,256]{2,1,0:T(8,128)(2,1)}, u32[]{:S(2)}, u32[]{:S(2)}) async-start(bf16[128,24,256]{2,1,0:T(8,128)(2,1)} %bitcast.54), calls=%async_computation.1 | async-start | bytes 3145728 | tf_op jit(solution)/shard_map/all_to_all | solution.py:76
  63.2 5.7 %copy-start.24 = (s32[256,16]{0,1:T(8,128)S(1)}, s32[256,16]{0,1:T(8,128)}, u32[]{:S(2)}) copy-start(s32[256,16]{0,1:T(8,128)} %param.19) | copy-start | bytes 49156
  63.2 5.9 %copy-start.25 = (s32[256,16]{0,1:T(8,128)S(1)}, s32[256,16]{0,1:T(8,128)}, u32[]{:S(2)}) copy-start(s32[256,16]{0,1:T(8,128)} %param.21) | copy-start | bytes 49156
  63.2 6.1 %copy-start.26 = (s32[256,16]{0,1:T(8,128)S(1)}, s32[256,16]{0,1:T(8,128)}, u32[]{:S(2)}) copy-start(s32[256,16]{0,1:T(8,128)} %param.20) | copy-start | bytes 49156
  63.2 6.3 %copy-start.27 = (s32[256,16]{0,1:T(8,128)S(1)}, s32[256,16]{0,1:T(8,128)}, u32[]{:S(2)}) copy-start(s32[256,16]{0,1:T(8,128)} %param.22) | copy-start | bytes 49156
  63.2 69.7 %all-to-all-start.2 = ((bf16[128,80,256]{2,1,0:T(8,128)(2,1)}), bf16[128,80,256]{2,1,0:T(8,128)(2,1)}, u32[]{:S(2)}, u32[]{:S(2)}) async-start(bf16[128,80,256]{2,1,0:T(8,128)(2,1)} %bitcast.51), calls=%async_computation.2 | async-start | bytes 10485760 | tf_op jit(solution)/shard_map/all_to_all | solution.py:76
  68.8 148.4 %all-gather.3.cloned.1.call-start = ((), (), s32[]{:S(2)}) async-start(), calls=%async_computation.7 | async-start | bytes 8650752 | tf_op jit(solution)/shard_map/all_gather | solution.py:72
  132.9 16.3 %copy-start.9 = (bf16[256,1024]{1,0:T(8,128)(2,1)S(1)}, bf16[256,1024]{1,0:T(8,128)(2,1)}, u32[]{:S(2)}) copy-start(bf16[256,1024]{1,0:T(8,128)(2,1)} %param.27) | copy-start | bytes 1572868
  149.2 4.7 %copy-start.37 = (bf16[1024,256]{1,0:T(8,128)(2,1)S(1)}, bf16[1024,256]{1,0:T(8,128)(2,1)}, u32[]{:S(2)}) copy-start(bf16[1024,256]{1,0:T(8,128)(2,1)} %param.29) | copy-start | bytes 1572868
  151.5 4.0 copy-start.6
  151.5 4.0 copy-start.8
  154.6 3.4 copy-start.14
  155.5 2.5 copy-start.29
  155.8 1.5 copy-start.20
  156.6 1.4 copy-start.41
  217.2 4.6 %copy-start.7 = (bf16[8192,512]{0,1:T(8,128)(2,1)S(1)}, bf16[8192,512]{0,1:T(8,128)(2,1)}, u32[]{:S(2)}) copy-start(bf16[8192,512]{0,1:T(8,128)(2,1)} %all-gather.3.cloned.1.call-done) | copy-start | bytes 25165828
  217.2 4.6 %copy-start.17 = (f32[256,256]{0,1:T(8,128)S(1)}, f32[256,256]{0,1:T(8,128)}, u32[]{:S(2)}) copy-start(f32[256,256]{0,1:T(8,128)} %copy-done.16) | copy-start | bytes 786436
  217.2 4.6 %copy-start.33 = (s32[256]{0:T(256)S(1)}, s32[256]{0:T(256)}, u32[]{:S(2)}) copy-start(s32[256]{0:T(256)} %param.23) | copy-start | bytes 3076
  221.9 2.0 copy-start.30
  221.9 2.0 copy-start.31
  221.9 2.1 copy-start.36
  221.9 2.1 copy-start.42
  224.0 1.7 copy-start.22
  224.0 1.7 copy-start.32
  226.3 12.9 %all-to-all-start.3 = ((f32[32,2,256]{2,1,0:T(2,128)}), f32[32,2,256]{2,1,0:T(2,128)S(1)}, u32[]{:S(2)}, u32[]{:S(2)}) async-start(f32[32,2,256]{2,1,0:T(2,128)} %broadcast_in_dim.2), calls=%async_computation.3 | async-start | bytes 131072 | tf_op jit(solution)/shard_map/all_to_all | solution.py:388
  239.3 6.7 %copy-start.15 = (f32[256,256]{0,1:T(8,128)S(1)}, f32[256,256]{0,1:T(8,128)}, u32[]{:S(2)}) copy-start(f32[256,256]{0,1:T(8,128)} %copy-done.14) | copy-start | bytes 786436
  239.3 6.7 %copy-start.28 = (f32[256]{0:T(256)S(1)}, f32[256]{0:T(256)}, u32[]{:S(2)}) copy-start(f32[256]{0:T(256)} %get-tuple-element.79) | copy-start | bytes 3076
  239.3 6.8 %copy-start.38 = (bf16[1024,256]{1,0:T(8,128)(2,1)S(1)}, bf16[1024,256]{1,0:T(8,128)(2,1)}, u32[]{:S(2)}) copy-start(bf16[1024,256]{1,0:T(8,128)(2,1)} %param.29) | copy-start | bytes 1572868
  246.1 2.3 copy-start.40
  246.1 2.9 copy-start.19
  248.4 1.6 copy-start.34
  250.0 1.4 copy-start.44
  251.3 4.5 copy-start.12
  251.3 1.5 copy-start.43
  251.3 2.1 copy-start.10
  254.0 2.4 copy-start.2
  255.4 4.9 %collective-permute-start = (bf16[512,1536]{1,0:T(8,128)(2,1)}, bf16[512,1536]{1,0:T(8,128)(2,1)}, u32[]{:S(2)}, u32[]{:S(2)}) collective-permute-start(bf16[512,1536]{1,0:T(8,128)(2,1)} %constant_dynamic-slice_fusion.1), channel_id=1, source_target_pairs={{0,1},{1,0},{2,3},{3,2},{4,5},{5,4},{6,7},{7,6},{8,9},{9,8},{10,11... | collective-permute-start | bytes 4718600 | tf_op jit(solution)/shard_map/ppermute | solution.py:83
  256.5 2.2 copy-start.4
  256.5 2.3 copy-start.11
  256.5 2.6 copy-start.13
  258.6 4.0 collective-permute-start.1
  258.8 2.1 copy-start.3
  259.5 3.2 copy-start.5
  266.6 47.1 %all-to-all-start.4 = ((bf16[64,8,3072]{2,1,0:T(8,128)(2,1)}), bf16[64,8,3072]{2,1,0:T(8,128)(2,1)}, u32[]{:S(2)}, u32[]{:S(2)}) async-start(bf16[64,8,3072]{2,1,0:T(8,128)(2,1)} %pad_maximum_fusion.2), calls=%async_computation.4 | async-start | bytes 6291456 | tf_op jit(solution)/shard_map/all_to_all | solution.py:90
  273.2 171.4 %all-gather.5.cloned.1.call-start = ((), (), s32[]{:S(2)}) async-start(), calls=%async_computation.8 | async-start | bytes 6340608 | tf_op jit(solution)/shard_map/all_gather | solution.py:95
  391.1 31.9 %all-to-all-start.6 = ((bf16[128,24,256]{2,1,0:T(8,128)(2,1)}), bf16[128,24,256]{2,1,0:T(8,128)(2,1)S(1)}, u32[]{:S(2)}, u32[]{:S(2)}) async-start(bf16[128,24,256]{2,1,0:T(8,128)(2,1)} %bitcast.16), calls=%async_computation.6 | async-start | bytes 3145728 | tf_op jit(solution)/shard_map/all_to_all | solution.py:76
  444.6 9.5 %copy-start.1 = (bf16[1024,1024]{1,0:T(8,128)(2,1)S(1)}, bf16[1024,1024]{1,0:T(8,128)(2,1)}, u32[]{:S(2)}) copy-start(bf16[1024,1024]{1,0:T(8,128)(2,1)} %param.25) | copy-start | bytes 6291460
  (6 other events, 6.1 us)
Sparse Core Ops, SparseCore 0:
  158.9 58.2 all-gather.2
  316.8 127.8 all-gather.4

commit v4 on v3

--- a/solution.py
+++ b/solution.py
@@ -393,11 +393,11 @@
         tiled=True,
     )
     query_back, query_backs = tower_backward(d_query, query_saved, query_w1, query_w2, query_w3)
-    told_all, query_backs = lax.optimization_barrier((told_all, query_backs))
+    weights_t = score_weights(item_unit, queries_all)
+    told_all, query_backs, weights_t = lax.optimization_barrier((told_all, query_backs, weights_t))
     query_terms = core_sum(weight_grads(pooled_query, query_saved, query_backs))
     inverse_all, positive_all = (told_all[:, i, :].reshape(1, -1) for i in range(2))
     own = lax.axis_index(GROUP_AXES) * examples + jnp.arange(examples, dtype=jnp.int32)
-    weights_t = score_weights(item_unit, queries_all)
     target_t = (positive_all == own[:, None].astype(jnp.float32)).astype(jnp.float32)
     d_item = SCALE * jnp.dot(
         (weights_t * inverse_all - target_t).astype(jnp.bfloat16),

time: 462 us -> 471 us (1.019)
  matrix products: 36 us -> 45 us
    dot_general x7 -> x8, matrix products: 13.4 us -> 18.6 us  [outer_t(): lax.dot_general(left, right, (((1,), (1,)), ((), ())), preferred_element_...]
    dot_general x1, matrix products: 1.96 us -> 6.69 us  [local(): jnp.dot((weights * inverse - target).astype(jnp.bfloat16), items_all, pre...]
    unnamed x98 -> x92, local copies, waits for them, and re-layouts: 8.26 us -> 9.44 us
  transfers between devices with their start and end apart: 9 -> 9, of which waited for: 6 -> 6; matrix products, arithmetic and copies ran while one was open for 3% -> 5% of each run, Pallas kernels for 17% -> 16%
where the time goes in v4:
time: 471 us; the launch traced here: 470 us
  waiting for transfers between devices  158 us (34%)
  blocking collectives  94 us (20%)
  Pallas kernels  93.3 us (20%)
  matrix products  45 us (10%)
  starting transfers between devices  32 us (7%)
  local copies, waits for them, and re-layouts  21.4 us (5%)
  between operations  14.8 us (3%)
  other arithmetic  12.4 us (3%)
    all_to_all x2, blocking collectives, exchange(): lax.all_to_all(rows, MESH_AXES, split_axis=0, concat_axis=0, tiled=True)  94 us
    all_to_all x3, waiting for transfers between devices, exchange(): lax.all_to_all(rows, MESH_AXES, split_axis=0, concat_axis=0, tiled=True)  77.6 us
    all_gather x1, waiting for transfers between devices, gather_group(): return lax.all_gather(values, GROUP_AXES, axis=0, tiled=True)  58.4 us
    pallas_call x2, Pallas kernels, spread_rows(): pl.pallas_call(spread_kernel, out_shape=jax.ShapeDtypeStruct((rows, featu...  40.4 us
    pallas_call x1, Pallas kernels, absorb_rows(): pl.pallas_call(functools.partial(absorb_kernel, steps, batch, unroll), gr...  21.6 us
    all_gather x1, waiting for transfers between devices, gather_rows(): return lax.all_gather(part, ('core', *CHIP_AXES), axis=0, tiled=True)  20.5 us
    dot_general x8, matrix products, outer_t(): lax.dot_general(left, right, (((1,), (1,)), ((), ())), preferred_element_...  18.6 us
    pallas_call x1, Pallas kernels, pool_rows(): pl.pallas_call(pool_kernel, out_shape=jax.ShapeDtypeStruct((examples, fea...  16.3 us
  transfers between devices with their start and end apart: 9, of which 6 were waited for; matrix products, arithmetic and copies ran while one was open for 5% of the time, Pallas kernels for 16%

profile of v4, /device:TPU:1, one launch (start us, length us, event | category | flops | bytes accessed | tf_op | source)
XLA Modules:
  0.0 470.4 jit_solution(5943705084008813205)
XLA Ops:
  7.2 1.0 copy.60
  8.1 0.9 copy.59
  9.1 20.8 %all_to_all.42 = s32[128,1,104]{2,1,0:T(1,128)S(1)} all-to-all(s32[128,1,104]{2,1,0:T(1,128)S(1)} %bitcast.59), channel_id=1, replica_groups=mesh['grp'=4,'z'=4,'x'=4,'core'=2] {'grp','z','x','core'}, dimensions={0} | all-to-all | bytes 106496 | tf_op jit(solution)/shard_map/all_to_all | solution.py:76
  30.1 3.1 convolution_convert_fusion
  33.1 5.3 %all-to-all-start.1 = ((bf16[128,24,256]{2,1,0:T(8,128)(2,1)}), bf16[128,24,256]{2,1,0:T(8,128)(2,1)}, u32[]{:S(2)}, u32[]{:S(2)}) async-start(bf16[128,24,256]{2,1,0:T(8,128)(2,1)} %bitcast.55), calls=%async_computation.1 | async-start | bytes 3145728 | tf_op jit(solution)/shard_map/all_to_all | solution.py:76
  39.2 14.9 %pick_rows.1 = bf16[10240,256]{1,0:T(8,128)(2,1)} custom-call(s32[10240]{0:T(1024)} %mul.348.place_ref, bf16[8192,256]{1,0:T(8,128)(2,1)} %table_ref.1), custom_call_target="tpu_custom_call" | custom-call | bytes 43200000 | tf_op jit(solution)/shard_map/pick_rows/pallas_call | solution.py:170
  54.0 9.2 %all-to-all-done.1 = bf16[128,24,256]{2,1,0:T(8,128)(2,1)} async-done(((bf16[128,24,256]{2,1,0:T(8,128)(2,1)}), bf16[128,24,256]{2,1,0:T(8,128)(2,1)}, u32[]{:S(2)}, u32[]{:S(2)}) %all-to-all-start.1) | async-done | bytes 1572896 | tf_op jit(solution)/shard_map/all_to_all | solution.py:76
  63.2 5.6 %all-to-all-start.2 = ((bf16[128,80,256]{2,1,0:T(8,128)(2,1)}), bf16[128,80,256]{2,1,0:T(8,128)(2,1)}, u32[]{:S(2)}, u32[]{:S(2)}) async-start(bf16[128,80,256]{2,1,0:T(8,128)(2,1)} %bitcast.52), calls=%async_computation.2 | async-start | bytes 10485760 | tf_op jit(solution)/shard_map/all_to_all | solution.py:76
  70.4 62.5 %all-to-all-done.2 = bf16[128,80,256]{2,1,0:T(8,128)(2,1)} async-done(((bf16[128,80,256]{2,1,0:T(8,128)(2,1)}), bf16[128,80,256]{2,1,0:T(8,128)(2,1)}, u32[]{:S(2)}, u32[]{:S(2)}) %all-to-all-start.2) | async-done | bytes 5242912 | tf_op jit(solution)/shard_map/all_to_all | solution.py:76
  132.9 16.3 %pool_rows.1 = bf16[512,256]{1,0:T(8,128)(2,1)} custom-call(s32[8192]{0:T(1024)} %get-tuple-element.96.place_q_ref.place_ref.other_place_ref, s32[8192]{0:T(1024)} %get-tuple-element.97.place_r_ref.other_place_ref.place_ref, bf16[10240,256]{1,0:T(8,128)(2,1)} %bitcast.7.table_q_ref.other_ref, bf16[3072,256]{1,0:T(8,128)(2,1)} %bitcast.5.table_r_ref.other_ref), custom_call_target="tpu_custom_call" | custom-call | bytes 64800000 | tf_op jit(solution)/shard_map/pool_rows/pallas_call | solution.py:209
  149.2 1.2 fusion.49
  150.5 1.4 fusion.52
  151.9 1.0 copy-done.17
  152.9 0.8 fusion.55
  157.7 58.4 %all-gather.3.cloned.1.call-done = bf16[8192,512]{0,1:T(8,128)(2,1)} async-done(((bf16[256,512]{0,1:T(8,128)(2,1)}), bf16[8192,512]{0,1:T(8,128)(2,1)}) %all-gather.3.cloned.1.call-update) | async-done | bytes 8388624 | tf_op jit(solution)/shard_map/all_gather | solution.py:72
  216.1 7.7 %fusion.62 = (f32[256]{0:T(256)S(1)}, f32[256,8192]{1,0:T(8,128)}) fusion(bf16[256,256]{0,1:T(8,128)(2,1)S(1)} %multiply_convert_fusion.5, bf16[8192,512]{0,1:T(8,128)(2,1)} %all-gather.3.cloned.1.call-done), kind=kOutput, calls=%fused_computation.119 | convolution fusion | flops 1080033024 | bytes 12715008 | tf_op jit(solution)/shard_map/dot_general | solution.py:29
  224.4 5.6 %all-to-all-start.3 = ((f32[32,2,256]{2,1,0:T(2,128)}), f32[32,2,256]{2,1,0:T(2,128)S(1)}, u32[]{:S(2)}, u32[]{:S(2)}) async-start(f32[32,2,256]{2,1,0:T(2,128)} %broadcast_in_dim.2), calls=%async_computation.3 | async-start | bytes 131072 | tf_op jit(solution)/shard_map/all_to_all | solution.py:388
  230.1 6.7 %multiply_reduce_fusion.1 = (f32[256]{0:T(256)S(1)}, f32[256,256]{0,1:T(8,128)S(1)}) fusion(f32[256,256]{0,1:T(8,128)} %copy-done.15, bf16[8192,512]{0,1:T(8,128)(2,1)} %all-gather.3.cloned.1.call-done, f32[256,8192]{1,0:T(8,128)} %get-tuple-element.91, s32[256]{0:T(256)S(1)} %copy-done.28, f32[256]{0:T(256)S(1)} %broadcast_divide_fusion), kind=kOutput, calls=%fused_computation.85 | convolution fusion | flops 1084423936 | bytes 13110272 | tf_op jit(solution)/shard_map/dot_general | solution.py:382
  236.9 0.9 fusion.31
  237.8 5.2 %fusion.1 = f32[256,8192]{1,0:T(8,128)} fusion(bf16[256,256]{0,1:T(8,128)(2,1)S(1)} %multiply_convert_fusion.4, bf16[8192,512]{0,1:T(8,128)(2,1)S(1)} %copy-done.5), kind=kOutput, calls=%fused_computation.2 | convolution fusion | flops 1077936128 | bytes 12713984 | tf_op jit(solution)/shard_map/dot_general | solution.py:29
  243.0 2.1 fusion.24
  245.2 6.3 %multiply_reduce_fusion = (f32[256]{0:T(256)S(1)}, f32[256,256]{0,1:T(8,128)S(1)}) fusion(f32[256,256]{0,1:T(8,128)S(1)} %copy-done.14, bf16[8192,512]{0,1:T(8,128)(2,1)} %all-gather.3.cloned.1.call-done, f32[256,8192]{1,0:T(8,128)} %fusion.1, f32[8192]{0:T(1024)S(1)} %bitcast.63, f32[8192]{0:T(1024)S(1)} %bitcast.62, f32[256]{0:T(256)S(1)} %add_convert_fusion.2), kind=kOutput, calls=%fused_computation.83 | convolution fusion | flops 1084423936 | bytes 13174784 | tf_op jit(solution)/shard_map/dot_general | solution.py:402
  251.6 0.9 fusion.45
  253.5 1.3 fusion.38
  254.8 0.9 convolution_convert_fusion.1
  256.6 1.3 constant_dynamic-slice_fusion
  260.1 0.9 convolution_convert_fusion.2
  261.3 1.6 copy-done.3
  263.0 1.2 constant_dynamic-slice_fusion.1
  265.3 0.8 pad_maximum_fusion.3.back_ref
  266.2 2.6 fusion.17
  268.7 1.8 fusion.16
  270.5 2.1 pad_maximum_fusion.2
  272.6 10.2 %all-to-all-start.4 = ((bf16[64,8,3072]{2,1,0:T(8,128)(2,1)}), bf16[64,8,3072]{2,1,0:T(8,128)(2,1)}, u32[]{:S(2)}, u32[]{:S(2)}) async-start(bf16[64,8,3072]{2,1,0:T(8,128)(2,1)} %pad_maximum_fusion.2), calls=%async_computation.4 | async-start | bytes 6291456 | tf_op jit(solution)/shard_map/all_to_all | solution.py:90
  282.9 22.0 %spread_rows.2 = bf16[10240,256]{1,0:T(8,128)(2,1)} custom-call(s32[8192]{0:T(1024)} %get-tuple-element.96.place_q_ref.place_ref.other_place_ref, s32[8192]{0:T(1024)} %get-tuple-element.97.place_r_ref.other_place_ref.place_ref, bf16[3072,256]{1,0:T(8,128)(2,1)} %bitcast.5.table_r_ref.other_ref, f32[512,256]{1,0:T(8,128)} %pad_maximum_fusion.3.back_ref), custom_call_target="tpu_custom_call" | custom-call | bytes 90000000 | tf_op jit(solution)/shard_map/spread_rows/pallas_call | solution.py:258
  304.9 18.4 %spread_rows.3 = bf16[3072,256]{1,0:T(8,128)(2,1)} custom-call(s32[8192]{0:T(1024)} %get-tuple-element.97.place_r_ref.other_place_ref.place_ref, s32[8192]{0:T(1024)} %get-tuple-element.96.place_q_ref.place_ref.other_place_ref, bf16[10240,256]{1,0:T(8,128)(2,1)} %bitcast.7.table_q_ref.other_ref, f32[512,256]{1,0:T(8,128)} %pad_maximum_fusion.3.back_ref), custom_call_target="tpu_custom_call" | custom-call | bytes 90000000 | tf_op jit(solution)/shard_map/spread_rows/pallas_call | solution.py:258
  323.3 1.0 all-to-all-done.4
  324.4 3.0 reduce_sum.62
  327.4 73.2 %all_to_all.43 = bf16[128,80,256]{2,1,0:T(8,128)(2,1)} all-to-all(bf16[128,80,256]{2,1,0:T(8,128)(2,1)} %bitcast.53), channel_id=1, replica_groups=mesh['grp'=4,'z'=4,'x'=4,'core'=2] {'grp','z','x','core'}, dimensions={0} | all-to-all | bytes 10485760 | tf_op jit(solution)/shard_map/all_to_all | solution.py:76
  400.6 4.4 all-to-all-start.6
  405.0 21.6 %absorb_rows.1 = f32[8192,256]{1,0:T(8,128)} custom-call(s32[10240]{0:T(1024)} %mul.348.place_ref, bf16[10240,256]{1,0:T(8,128)(2,1)} %bitcast.54), custom_call_target="tpu_custom_call" | custom-call | bytes 79200000 | tf_op jit(solution)/shard_map/absorb_rows/pallas_call | solution.py:313
  426.6 5.9 %all-to-all-done.6 = bf16[128,24,256]{2,1,0:T(8,128)(2,1)S(1)} async-done(((bf16[128,24,256]{2,1,0:T(8,128)(2,1)}), bf16[128,24,256]{2,1,0:T(8,128)(2,1)S(1)}, u32[]{:S(2)}, u32[]{:S(2)}) %all-to-all-start.6) | async-done | bytes 1572896 | tf_op jit(solution)/shard_map/all_to_all | solution.py:76
  432.5 1.1 fusion.15
  433.6 20.5 %all-gather.5.cloned.1.call-done = bf16[1024,3072]{1,0:T(8,128)(2,1)} async-done(((bf16[8,3072]{1,0:T(8,128)(2,1)}), bf16[1024,3072]{1,0:T(8,128)(2,1)}) %all-gather.5.cloned.1.call-update) | async-done | bytes 6291472 | tf_op jit(solution)/shard_map/all_gather | solution.py:95
  454.1 2.6 fusion.59
  456.7 4.8 %fusion.60 = (bf16[1024,1024]{1,0:T(8,128)(2,1)}, bf16[1024,1024]{1,0:T(8,128)(2,1)}) fusion(bf16[1024,3072]{1,0:T(8,128)(2,1)} %all-gather.5.cloned.1.call-done), kind=kLoop, calls=%fused_computation.117 | loop fusion | bytes 8388608 | tf_op jit(solution)/shard_map/split | solution.py:427
  461.5 1.0 copy.71
  462.5 1.0 copy.72
  (129 shorter events, 12.7 us)
Async XLA Ops:
  7.2 145.7 %copy-start = (bf16[1024,1024]{1,0:T(8,128)(2,1)S(1)}, bf16[1024,1024]{1,0:T(8,128)(2,1)}, u32[]{:S(2)}) copy-start(bf16[1024,1024]{1,0:T(8,128)(2,1)} %param.25) | copy-start | bytes 6291460
  33.1 30.1 %all-to-all-start.1 = ((bf16[128,24,256]{2,1,0:T(8,128)(2,1)}), bf16[128,24,256]{2,1,0:T(8,128)(2,1)}, u32[]{:S(2)}, u32[]{:S(2)}) async-start(bf16[128,24,256]{2,1,0:T(8,128)(2,1)} %bitcast.55), calls=%async_computation.1 | async-start | bytes 3145728 | tf_op jit(solution)/shard_map/all_to_all | solution.py:76
  63.2 5.7 %copy-start.24 = (s32[256,16]{0,1:T(8,128)S(1)}, s32[256,16]{0,1:T(8,128)}, u32[]{:S(2)}) copy-start(s32[256,16]{0,1:T(8,128)} %param.21) | copy-start | bytes 49156
  63.2 5.9 %copy-start.25 = (s32[256,16]{0,1:T(8,128)S(1)}, s32[256,16]{0,1:T(8,128)}, u32[]{:S(2)}) copy-start(s32[256,16]{0,1:T(8,128)} %param.19) | copy-start | bytes 49156
  63.2 6.1 %copy-start.26 = (s32[256,16]{0,1:T(8,128)S(1)}, s32[256,16]{0,1:T(8,128)}, u32[]{:S(2)}) copy-start(s32[256,16]{0,1:T(8,128)} %param.22) | copy-start | bytes 49156
  63.2 6.3 %copy-start.27 = (s32[256,16]{0,1:T(8,128)S(1)}, s32[256,16]{0,1:T(8,128)}, u32[]{:S(2)}) copy-start(s32[256,16]{0,1:T(8,128)} %param.20) | copy-start | bytes 49156
  63.2 69.7 %all-to-all-start.2 = ((bf16[128,80,256]{2,1,0:T(8,128)(2,1)}), bf16[128,80,256]{2,1,0:T(8,128)(2,1)}, u32[]{:S(2)}, u32[]{:S(2)}) async-start(bf16[128,80,256]{2,1,0:T(8,128)(2,1)} %bitcast.52), calls=%async_computation.2 | async-start | bytes 10485760 | tf_op jit(solution)/shard_map/all_to_all | solution.py:76
  68.8 147.3 %all-gather.3.cloned.1.call-start = ((), (), s32[]{:S(2)}) async-start(), calls=%async_computation.7 | async-start | bytes 8650752 | tf_op jit(solution)/shard_map/all_gather | solution.py:72
  132.9 16.4 %copy-start.8 = (bf16[256,1024]{1,0:T(8,128)(2,1)S(1)}, bf16[256,1024]{1,0:T(8,128)(2,1)}, u32[]{:S(2)}) copy-start(bf16[256,1024]{1,0:T(8,128)(2,1)} %param.27) | copy-start | bytes 1572868
  132.9 17.6 %copy-start.7 = (bf16[256,1024]{1,0:T(8,128)(2,1)S(1)}, bf16[256,1024]{1,0:T(8,128)(2,1)}, u32[]{:S(2)}) copy-start(bf16[256,1024]{1,0:T(8,128)(2,1)} %param.24) | copy-start | bytes 1572868
  150.5 3.9 copy-start.20
  150.5 3.2 copy-start.31
  152.9 1.6 copy-start.29
  153.7 1.6 copy-start.35
  154.3 1.8 copy-start.15
  154.3 1.2 copy-start.33
  155.5 1.4 copy-start.38
  155.5 2.1 copy-start.28
  224.4 20.6 %all-to-all-start.3 = ((f32[32,2,256]{2,1,0:T(2,128)}), f32[32,2,256]{2,1,0:T(2,128)S(1)}, u32[]{:S(2)}, u32[]{:S(2)}) async-start(f32[32,2,256]{2,1,0:T(2,128)} %broadcast_in_dim.2), calls=%async_computation.3 | async-start | bytes 131072 | tf_op jit(solution)/shard_map/all_to_all | solution.py:388
  230.1 6.7 %copy-start.16 = (f32[256,256]{0,1:T(8,128)S(1)}, f32[256,256]{0,1:T(8,128)}, u32[]{:S(2)}) copy-start(f32[256,256]{0,1:T(8,128)} %copy-done.15) | copy-start | bytes 786436
  230.1 6.8 %copy-start.32 = (bf16[1024,256]{1,0:T(8,128)(2,1)S(1)}, bf16[1024,256]{1,0:T(8,128)(2,1)}, u32[]{:S(2)}) copy-start(bf16[1024,256]{1,0:T(8,128)(2,1)} %param.26) | copy-start | bytes 1572868
  230.1 6.8 %copy-start.36 = (f32[256,1024]{1,0:T(8,128)S(1)}, f32[256,1024]{1,0:T(8,128)}, u32[]{:S(2)}) copy-start(f32[256,1024]{1,0:T(8,128)} %copy-done.35) | copy-start | bytes 3145732
  230.1 7.7 %copy-start.5 = (bf16[8192,512]{0,1:T(8,128)(2,1)S(1)}, bf16[8192,512]{0,1:T(8,128)(2,1)}, u32[]{:S(2)}) copy-start(bf16[8192,512]{0,1:T(8,128)(2,1)} %all-gather.3.cloned.1.call-done) | copy-start | bytes 25165828
  237.8 5.2 %copy-start.40 = (bf16[256,1024]{1,0:T(8,128)(2,1)}, bf16[256,1024]{1,0:T(8,128)(2,1)S(1)}, u32[]{:S(2)}) copy-start(bf16[256,1024]{1,0:T(8,128)(2,1)S(1)} %fusion.31) | copy-start | bytes 1572868
  237.8 5.2 %copy-start.18 = (f32[256,1024]{1,0:T(8,128)S(1)}, f32[256,1024]{1,0:T(8,128)}, u32[]{:S(2)}) copy-start(f32[256,1024]{1,0:T(8,128)} %copy-done.17) | copy-start | bytes 3145732
  243.0 2.1 copy-start.14
  245.2 6.4 %copy-start.34 = (bf16[1024,256]{1,0:T(8,128)(2,1)S(1)}, bf16[1024,256]{1,0:T(8,128)(2,1)}, u32[]{:S(2)}) copy-start(bf16[1024,256]{1,0:T(8,128)(2,1)} %param.29) | copy-start | bytes 1572868
  245.2 6.4 %copy-start.39 = (f32[256,1024]{1,0:T(8,128)S(1)}, f32[256,1024]{1,0:T(8,128)}, u32[]{:S(2)}) copy-start(f32[256,1024]{1,0:T(8,128)} %copy-done.38) | copy-start | bytes 3145732
  251.6 1.5 copy-start.21
  251.6 1.9 copy-start.30
  254.8 1.8 copy-start.11
  254.8 1.1 copy-start.6
  256.5 3.3 copy-start.2
  256.6 1.7 copy-start.9
  256.6 2.1 copy-start.23
  256.6 2.7 copy-start.37
  256.6 3.4 copy-start.19
  256.6 3.5 copy-start.41
  257.9 8.3 %collective-permute-start.1 = (bf16[512,1536]{1,0:T(8,128)(2,1)}, bf16[512,1536]{1,0:T(8,128)(2,1)}, u32[]{:S(2)}, u32[]{:S(2)}) collective-permute-start(bf16[512,1536]{1,0:T(8,128)(2,1)} %constant_dynamic-slice_fusion), channel_id=1, source_target_pairs={{0,1},{1,0},{2,3},{3,2},{4,5},{5,4},{6,7},{7,6},{8,9},{9,8},{10,11... | collective-permute-start | bytes 4718600 | tf_op jit(solution)/shard_map/ppermute | solution.py:83
  261.3 1.6 copy-start.3
  263.0 1.7 copy-start.10
  263.0 2.0 copy-start.12
  264.2 4.5 collective-permute-start
  265.3 3.4 copy-start.4
  272.6 51.8 %all-to-all-start.4 = ((bf16[64,8,3072]{2,1,0:T(8,128)(2,1)}), bf16[64,8,3072]{2,1,0:T(8,128)(2,1)}, u32[]{:S(2)}, u32[]{:S(2)}) async-start(bf16[64,8,3072]{2,1,0:T(8,128)(2,1)} %pad_maximum_fusion.2), calls=%async_computation.4 | async-start | bytes 6291456 | tf_op jit(solution)/shard_map/all_to_all | solution.py:90
  282.9 171.2 %all-gather.5.cloned.1.call-start = ((), (), s32[]{:S(2)}) async-start(), calls=%async_computation.8 | async-start | bytes 6340608 | tf_op jit(solution)/shard_map/all_gather | solution.py:95
  400.6 31.9 %all-to-all-start.6 = ((bf16[128,24,256]{2,1,0:T(8,128)(2,1)}), bf16[128,24,256]{2,1,0:T(8,128)(2,1)S(1)}, u32[]{:S(2)}, u32[]{:S(2)}) async-start(bf16[128,24,256]{2,1,0:T(8,128)(2,1)} %bitcast.16), calls=%async_computation.6 | async-start | bytes 3145728 | tf_op jit(solution)/shard_map/all_to_all | solution.py:76
  456.7 6.8 %copy-start.1 = (bf16[1024,1024]{1,0:T(8,128)(2,1)S(1)}, bf16[1024,1024]{1,0:T(8,128)(2,1)}, u32[]{:S(2)}) copy-start(bf16[1024,1024]{1,0:T(8,128)(2,1)} %param.25) | copy-start | bytes 6291460
  (3 other events, 2.6 us)
Sparse Core Ops, SparseCore 0:
  157.7 58.2 all-gather.2
  327.5 126.5 all-gather.4
